TPU v7x, 768 devices: a whole 4x8x12 slice. The times are simulated.
768 devices in a mesh: ctx: 64 (over x, y, core), tp: 12 (over z).
Axes of the slice: x: 4, y: 8, z: 12, core: 2. Of those that a mesh axis runs over, the one named last changes fastest.
Arguments:
- tokens: bfloat16 [98304, 2048], P(('ctx', 'tp')), may hold values from -8 to 8
- projection: bfloat16 [2048, 1920], P(None, 'tp'), may hold values from -0.125 to 0.125
- conv_weight: float32 [4, 1920], P(None, 'tp'), may hold values from -2.5 to 2.5
Outputs:
- attended: bfloat16 [98304, 1536], P('ctx', 'tp')
All inputs are finite; a program needn't handle non-finite values.
Results may differ from a plain program's by a relative error of at most 0.0032.
The roundings to bfloat16 on the way count: a program that leaves them out, or rounds other values in their place, can miss the bound.
Values may be sent and summed in bfloat16 or wider, within the bound.
A program may use at most 64 MiB of HBM per device.

v0:
```python
import math

import jax
import jax.numpy as jnp
from jax import lax
from jax.sharding import PartitionSpec as P

FEAT = 16


def passed_along(shard, axis, by):
    length = lax.axis_size(axis)
    pairs = [(i, i + by) for i in range(length) if 0 <= i + by < length]
    return lax.ppermute(shard, axis, pairs)


def taylor(raw_vals):
    num_rows, width_feat = raw_vals.shape
    linear = raw_vals * width_feat ** (-0.25)
    quadratic = (raw_vals[:, :, None] * raw_vals[:, None, :]).reshape(
        num_rows, width_feat * width_feat
    )
    quadratic = quadratic * (1.0 / (math.sqrt(2.0) * math.sqrt(width_feat)))
    ones_col = jnp.ones((num_rows, 1), jnp.float32)
    return jnp.concatenate([ones_col, linear, quadratic], axis=1).astype(jnp.bfloat16)


def per_device(tokens, projection, conv_weight):
    kernel_len = conv_weight.shape[0]
    conv_lag = kernel_len - 1
    row_width = projection.shape[1]
    highest = lax.Precision.HIGHEST
    projected = jnp.dot(
        lax.all_gather(tokens, "tp", axis=0, tiled=True),
        projection,
        preferred_element_type=jnp.float32,
    ).astype(jnp.bfloat16)
    rim_rows = passed_along(projected[projected.shape[0] - conv_lag :], "ctx", 1)
    local_rows = projected.shape[0]
    padded = jnp.concatenate([rim_rows, projected], axis=0).astype(jnp.float32)
    convolved = jnp.zeros((local_rows, row_width), jnp.float32)
    for offset in range(kernel_len):
        convolved = (
            convolved
            + conv_weight[offset] * padded[conv_lag - offset : conv_lag - offset + local_rows]
        )
    feat_query = taylor(convolved[:, :FEAT])
    feat_key = taylor(convolved[:, FEAT : 2 * FEAT])
    values = convolved[:, 2 * FEAT :].astype(jnp.bfloat16)
    num_feat = feat_key.shape[1]
    val_width = values.shape[1]
    local_state = jnp.einsum("tp,tv->pv", feat_key, values, preferred_element_type=jnp.float32)
    local_total = jnp.sum(feat_key.astype(jnp.float32), axis=0)
    empty_state = jnp.zeros((num_feat, val_width), jnp.float32)
    empty_total = jnp.zeros((num_feat,), jnp.float32)
    position = lax.axis_index("ctx")
    states = lax.all_gather(local_state[None], "ctx", axis=0, tiled=True)
    sums = lax.all_gather(local_total[None], "ctx", axis=0, tiled=True)
    earlier_mask = jnp.arange(states.shape[0]) < position
    new_state = jnp.sum(jnp.where(earlier_mask[:, None, None], states, 0.0), axis=0)
    new_total = jnp.sum(jnp.where(earlier_mask[:, None], sums, 0.0), axis=0)
    block_rows = min(local_rows, 768)
    num_blocks = local_rows // block_rows
    query_blocks = feat_query.reshape(num_blocks, block_rows, num_feat)
    key_blocks = feat_key.reshape(num_blocks, block_rows, num_feat)
    value_blocks = values.reshape(num_blocks, block_rows, val_width)
    causal = jnp.arange(block_rows)[:, None] >= jnp.arange(block_rows)[None, :]

    def block_step(carried, blocks):
        run_state, run_total = carried
        query_blk, key_blk, value_blk = blocks
        scores = jnp.einsum("ip,jp->ij", query_blk, key_blk, preferred_element_type=jnp.float32)
        scores = jnp.where(causal, scores, 0.0)
        numerator = jnp.dot(
            scores.astype(jnp.bfloat16), value_blk, preferred_element_type=jnp.float32
        )
        denominator = jnp.sum(scores, axis=1)
        query_wide = query_blk.astype(jnp.float32)
        numerator = numerator + jnp.dot(query_wide, run_state, precision=highest)
        denominator = denominator + jnp.dot(query_wide, run_total, precision=highest)
        run_state = run_state + jnp.einsum(
            "tp,tv->pv", key_blk, value_blk, preferred_element_type=jnp.float32
        )
        run_total = run_total + jnp.sum(key_blk.astype(jnp.float32), axis=0)
        return ((run_state, run_total), (numerator, denominator))

    _, (numerator, denominator) = lax.scan(
        block_step, (empty_state, empty_total), (query_blocks, key_blocks, value_blocks)
    )
    numerator = numerator.reshape(local_rows, val_width)
    denominator = denominator.reshape(local_rows)
    query_wide = feat_query.astype(jnp.float32)
    numerator = numerator + jnp.dot(query_wide, new_state, precision=highest)
    denominator = denominator + jnp.dot(query_wide, new_total, precision=highest)
    return (numerator / denominator[:, None]).astype(jnp.bfloat16)


def solution(mesh):
    return jax.shard_map(
        per_device,
        mesh=mesh,
        in_specs=(P(("ctx", "tp"), None), P(None, "tp"), P(None, "tp")),
        out_specs=P("ctx", "tp"),
        check_vma=False,
    )
```

profile of v0, /device:TPU:1, one launch (start us, length us, event | category | flops | bytes accessed | tf_op | source)
XLA Modules:
  0.0 414.9 jit_solution(5852287572250405038)
XLA Ops:
  6.5 0.7 all-gather.6.cloned.1.call-update
  7.3 94.5 %all-gather.6.cloned.1.call-done = bf16[1536,2048]{1,0:T(8,128)(2,1)} async-done(((bf16[128,2048]{1,0:T(8,128)(2,1)}), bf16[1536,2048]{1,0:T(8,128)(2,1)}) %all-gather.6.cloned.1.call-update) | async-done | bytes 6291472 | tf_op jit(solution)/shard_map/all_gather | solution.py:34
  101.8 5.0 %convolution_convert_fusion = bf16[1536,160]{0,1:T(8,128)(2,1)S(1)} fusion(bf16[1536,2048]{1,0:T(8,128)(2,1)} %all-gather.6.cloned.1.call-done, bf16[2048,160]{0,1:T(8,128)(2,1)S(1)} %copy-done), kind=kOutput, calls=%fused_computation.42 | convolution fusion | flops 1006878720 | bytes 7438336 | tf_op jit(solution)/shard_map/dot_general | solution.py:33
  106.9 3.7 collective-permute-start
  110.7 1.3 dynamic-slice
  112.8 1.0 fusion.37
  114.8 0.6 copy-done.3
  115.7 1.1 convolution_bitcast_fusion
  117.5 1.1 mul.117
  118.5 0.8 slice.76
  119.5 1.2 mul.123
  120.6 4.9 %pad_maximum_fusion.3 = (bf16[2,768,273]{1,0,2:T(2,128)(2,1)}, bf16[2,768,273]{1,0,2:T(2,128)(2,1)S(1)}) fusion(bf16[2,768,256]{1,0,2:T(2,128)(2,1)} %mul.123, bf16[2,768,16]{1,0,2:T(2,128)(2,1)S(1)} %concatenate.29, bf16[273]{0:T(512)(128)(2,1)S(1)} %pad.9.clone, bf16[2,768,256]{1,0,2:T(2,128)(2,1)} %mul.117, bf16[2,768,16]{1,0,2:T(2,128)(2,1)S(1)} %concatenate.27), kind=kLoop, calls=%fused_computation.59 | loop fusion | flops 1677312 | bytes 3349026 | tf_op jit(solution)/shard_map/concatenate | solution.py:25
  125.5 1.1 copy.19
  126.6 2.4 copy.21
  129.0 1.2 copy.22
  130.3 11.4 %while.17 = (s32[]{:T(128)}, f32[273,128]{1,0:T(8,128)S(1)}, f32[273]{0:T(512)}, f32[2,768,128]{2,1,0:T(8,128)}, f32[2,768]{1,0:T(2,128)}, /*index=5*/bf16[2,768...) while((s32[]{:T(128)}, f32[273,128]{1,0:T(8,128)S(1)}, ...), condition=%wide.region_3.4_spmd.clone, body=%wide.region_0.3_spmd.clone.sunk | while | flops 855434368 | bytes 14058645 | solution.py:87
  130.3 0.6 fusion.75
  130.9 0.8 fusion.76
  132.7 0.7 fusion.74
  134.0 1.3 dynamic_update_slice.14
  135.7 0.6 fusion.75
  136.3 0.8 fusion.76
  138.1 1.3 fusion.74
  140.0 1.3 dynamic_update_slice.14
  141.7 0.7 reshape.60
  142.4 162.6 %all-reduce.3.cloned.1.call-done = f32[17472]{0:T(1024)} async-done(((f32[17472]{0:T(1024)}), f32[17472]{0:T(1024)}) %all-reduce.3.cloned.1.call-update) | async-done | bytes 69904
  305.0 1.1 reshape.62
  306.1 0.7 select_reduce_fusion.1
  306.8 1.8 convolution_reduce_fusion.1
  308.6 92.7 %all-gather.8.cloned.1.call-done = f32[64,273,128]{2,1,0:T(8,128)} async-done(((f32[1,273,128]{2,1,0:T(8,128)}), f32[64,273,128]{2,1,0:T(8,128)}) %all-gather.8.cloned.1.call-update) | async-done | bytes 8945680 | tf_op jit(solution)/shard_map/all_gather | solution.py:57
  401.4 4.7 %select_reduce_fusion = f32[273,128]{1,0:T(8,128)S(1)} fusion(f32[64,273,128]{2,1,0:T(8,128)} %all-gather.8.cloned.1.call-done, pred[64]{0:T(512)(128)(4,1)S(1)} %copy-done.9), kind=kLoop, calls=%fused_computation.39 | loop fusion | flops 4437888 | bytes 9085504 | tf_op jit(solution)/shard_map/reduce_sum | solution.py:60
  406.1 2.3 fusion.36
  (68 shorter events, 6.2 us)
Async XLA Ops:
  6.5 95.3 %copy-start = (bf16[2048,160]{0,1:T(8,128)(2,1)S(1)}, bf16[2048,160]{0,1:T(8,128)(2,1)}, u32[]{:S(2)}) copy-start(bf16[2048,160]{0,1:T(8,128)(2,1)} %param.6) | copy-start | bytes 1966084
  6.5 95.3 %all-gather.6.cloned.1.call-start = ((), (), s32[]{:S(2)}) async-start(), calls=%async_computation | async-start | bytes 6815744 | tf_op jit(solution)/shard_map/all_gather | solution.py:34
  7.3 103.3 %copy-start.8 = (f32[4,160]{1,0:T(4,128)S(1)}, f32[4,160]{1,0:T(4,128)}, u32[]{:S(2)}) copy-start(f32[4,160]{1,0:T(4,128)} %param.7) | copy-start | bytes 7684
  7.3 297.7 %all-reduce.3.cloned.1.call-start = ((), (), s32[]{:S(2)}) async-start(), calls=%async_computation.1 | async-start | bytes 147456
  106.9 5.7 %collective-permute-start = (bf16[3,160]{0,1:T(8,128)(2,1)S(1)}, bf16[3,160]{0,1:T(8,128)(2,1)S(1)}, u32[]{:S(2)}, u32[]{:S(2)}) collective-permute-start(bf16[3,160]{0,1:T(8,128)(2,1)S(1)} %slice.49), channel_id=1, source_target_pairs={{0,12},{12,24},{24,36},{36,48},{48,60},{60,72},{72,84},{84,96},{96... | collective-permute-start | bytes 2888 | tf_op jit(solution)/shard_map/ppermute | solution.py:14
  110.6 10.0 %copy-start.6 = (bf16[273]{0:T(512)(128)(2,1)}, bf16[273]{0:T(512)(128)(2,1)S(1)}, u32[]{:S(2)}) copy-start(bf16[273]{0:T(512)(128)(2,1)S(1)} %pad.9.clone) | copy-start | bytes 1642
  113.9 5.4 %copy-start.4 = (bf16[1536,16]{0,1:T(8,128)(2,1)}, bf16[1536,16]{0,1:T(8,128)(2,1)S(1)}, u32[]{:S(2)}) copy-start(bf16[1536,16]{0,1:T(8,128)(2,1)S(1)} %get-tuple-element.136) | copy-start | bytes 147460
  114.8 0.6 copy-start.3
  115.5 285.9 %all-gather.8.cloned.1.call-start = ((), (), s32[]{:S(2)}) async-start(), calls=%async_computation.2 | async-start | bytes 9318400 | tf_op jit(solution)/shard_map/all_gather | solution.py:57
  119.5 6.0 %copy-start.1 = (bf16[1536,16,16]{0,2,1:T(8,128)(2,1)}, bf16[1536,16,16]{0,2,1:T(8,128)(2,1)S(1)}, u32[]{:S(2)}) copy-start(bf16[1536,16,16]{0,2,1:T(8,128)(2,1)S(1)} %multiply_convert_fusion) | copy-start | bytes 2359300
  130.9 1.1 copy-start.10
  132.5 1.5 copy-start.11
  136.3 1.1 copy-start.10
  138.0 2.1 copy-start.11
  141.7 259.7 %copy-start.9 = (pred[64]{0:T(512)(128)(4,1)S(1)}, pred[64]{0:T(512)(128)(4,1)}, u32[]{:S(2)}) copy-start(pred[64]{0:T(512)(128)(4,1)} %iota_compare_fusion.1) | copy-start | bytes 196
  308.6 97.5 %copy-start.2 = (bf16[1536,16,16]{0,2,1:T(8,128)(2,1)S(1)}, bf16[1536,16,16]{0,2,1:T(8,128)(2,1)}, u32[]{:S(2)}) copy-start(bf16[1536,16,16]{0,2,1:T(8,128)(2,1)} %copy-done.1) | copy-start | bytes 2359300
  308.6 97.4 %copy-start.5 = (bf16[1536,16]{0,1:T(8,128)(2,1)S(1)}, bf16[1536,16]{0,1:T(8,128)(2,1)}, u32[]{:S(2)}) copy-start(bf16[1536,16]{0,1:T(8,128)(2,1)} %copy-done.4) | copy-start | bytes 147460
  308.6 97.4 %copy-start.7 = (bf16[273]{0:T(512)(128)(2,1)S(1)}, bf16[273]{0:T(512)(128)(2,1)}, u32[]{:S(2)}) copy-start(bf16[273]{0:T(512)(128)(2,1)} %copy-done.6) | copy-start | bytes 1642
  308.6 97.4 %copy-start.12 = (f32[2,768,128]{2,1,0:T(8,128)S(1)}, f32[2,768,128]{2,1,0:T(8,128)}, u32[]{:S(2)}) copy-start(f32[2,768,128]{2,1,0:T(8,128)} %get-tuple-element.53) | copy-start | bytes 2359300
Sparse Core Ops, SparseCore 0:
  9.7 92.0 all-gather.5
  115.6 189.3 all-reduce.2
  308.8 92.4 all-gather.7
where the time goes:
time: 416 us; the launch traced here: 415 us
  waiting for transfers between devices  351 us (84%)
  matrix products  16 us (4%)
  local copies, waits for them, and re-layouts  15.2 us (4%)
  other arithmetic  15 us (4%)
  between operations  14.1 us (3%)
    unnamed x4, waiting for transfers between devices  163 us
    all_gather x1, waiting for transfers between devices, per_device(): lax.all_gather(tokens, 'tp', axis=0, tiled=True)  94.5 us
    all_gather x1, waiting for transfers between devices, per_device(): states = lax.all_gather(local_state[None], 'ctx', axis=0, tiled=True)  92.7 us
  transfers between devices with their start and end apart: 4, of which 3 were waited for; matrix products, arithmetic and copies ran while one was open for 7% of the time, Pallas kernels for 0%

commit v1 on v0

v1 whole, which is shorter than its diff:
```python
import jax
import jax.numpy as jnp
from jax import lax
from jax.experimental import pallas as pl
from jax.experimental.pallas import tpu as pltpu
from jax.sharding import PartitionSpec as P

NX, NY, NZ = 4, 8, 12
D = 2048
FEAT = 16
VW = 128
TILE = 128
ROWS = TILE * NZ
PACK = TILE // 4
PHI = 160
HALF = PHI // 2
TOT = 153
BLOCK = 768
SUB = 256
MESH = pl.DeviceIdType.MESH
bf16, f32 = jnp.bfloat16, jnp.float32


def kernel(tok_ref, proj_ref, conv_ref, out_ref,
           tokbuf, sa, sb, wa, wb, stage, xr, vb, fq, fk, st, loc, px, ch, ybuf, tx, xbuf, snd, fin, num, den,
           tk_s, tk_r, zs, zr, xs_s, xs_r, ya_s, ya_r, yb_s, yb_r, xb_s, xb_r, at_s, at_r, h_s, h_r,
           d1_s, d1_r, sy_s, sy_r, sx_s, sx_r, d2_s, d2_r):
    c = lax.axis_index("ctx")
    z = lax.axis_index("tp")
    r = lax.rem(c, 2)
    y = lax.rem(c // 2, NY)
    x = c // (2 * NY)

    def at(xx, yy, rr, zz):
        return ((xx * NY + yy) * 2 + rr, zz)

    def xo(d):
        return lax.rem(x + d + NX, NX)

    def yo(d):
        return lax.rem(y + d + NY, NY)

    def zo(d):
        return lax.rem(z + d + NZ, NZ)

    def copy(src, dst, ss, rs, dev):
        return pltpu.make_async_remote_copy(
            src_ref=src, dst_ref=dst, send_sem=ss, recv_sem=rs, device_id=dev, device_id_type=MESH)

    barrier = pltpu.get_barrier_semaphore()

    def greet(dev):
        pl.semaphore_signal(barrier, inc=1, device_id=dev, device_id_type=MESH)

    greet(at(x, y, 1 - r, z))
    for d in range(1, NX):
        greet(at(xo(d), y, r, z))
    for d in range(1, NY):
        greet(at(x, yo(d), r, z))
    for d in range(1, NZ):
        greet(at(x, y, r, zo(d)))
        greet(at(x, y, 1 - r, zo(d)))
    halo_in = jnp.logical_and(r == 0, c > 0)

    @pl.when(halo_in)
    def _():
        greet((c - 1, z))

    def value_rows(start, n):
        a = proj_ref[pl.ds(pl.multiple_of(start, 16), n), 0:128]
        b = proj_ref[pl.ds(pl.multiple_of(start, 16), n), 128:160]
        return jnp.concatenate([a[:, 32:], b], axis=1)

    def packed_rows(start, n):
        return jnp.concatenate(
            [proj_ref[pl.ds(pl.multiple_of(j * 512 + start, 16), n), 0:32] for j in range(4)], axis=1)

    for g in range(4):
        sa[g] = value_rows(y * 256 + g * 64 + x * 16, 16)
    sa[4] = packed_rows(y * 64 + x * 16, 16)
    ypar = lax.rem(y, 2)
    for g in range(4):
        sb[g] = value_rows(x * 512 + g * 128 + ypar * 64, 64)
    sb[4] = packed_rows(x * 128 + ypar * 64, 64)
    own_rows = pl.ds(pl.multiple_of(r * TILE, TILE), TILE)
    tokbuf[own_rows, :] = tok_ref[...]

    pl.semaphore_wait(barrier, NX + NY - 1 + 2 * (NZ - 1) + r * (1 - c // (2 * NX * NY - 1)))

    sends = []

    def dist(k):
        return jnp.where(r == 0, 6 - k, k - 6 if k else 0)

    xpiece = pl.ds(pl.multiple_of(x * 16, 16), 16)
    ypiece = pl.ds(pl.multiple_of(ypar * 64, 64), 64)

    def z_copy(k):
        i = k // 2
        dev = at(x, y, r, zo(-dist(k)))
        if k % 2 == 0:
            return copy(sa, wa.at[i, y, :, xpiece, :], zs.at[k], zr.at[k], dev)
        return copy(sb, wb.at[i, x, :, ypiece, :], zs.at[k], zr.at[k], dev)

    tok_copy = copy(tok_ref, tokbuf.at[own_rows, :], tk_s, tk_r, at(x, y, 1 - r, z))
    z_copies = [z_copy(k) for k in range(6)]

    @pl.when(r == 0)
    def _():
        z_copies[0].start()

    @pl.when(r == 1)
    def _():
        wa[0, y, :, xpiece, :] = sa[...]

    for k in range(1, 6):
        z_copies[k].start()
    tok_copy.start()
    sends.append(tok_copy)
    sends.extend(z_copies[1:])

    xs = {}
    pair = {}
    ring = {}
    xb = {}

    def a_small(i):
        if i == 0:
            @pl.when(r == 0)
            def _():
                z_copies[0].wait_recv()
        else:
            z_copies[2 * i].wait_recv()
        for d in range(1, NX):
            ref = wa.at[i, y, :, xpiece, :]
            cp = copy(ref, ref, xs_s.at[i, d - 1], xs_r.at[i, d - 1], at(xo(d), y, r, z))
            cp.start()
            xs[i, d] = cp
            sends.append(cp)

    def b_small(i):
        z_copies[2 * i + 1].wait_recv()
        ref = wb.at[i, x, :, ypiece, :]
        cp = copy(ref, ref, yb_s.at[i], yb_r.at[i], at(x, y + 1 - 2 * ypar, r, z))
        cp.start()
        pair[i] = cp
        sends.append(cp)

    def b_large(i):
        pair[i].wait_recv()
        for d in range(1, NX):
            ref = wb.at[i, x]
            cp = copy(ref, ref, xb_s.at[i, d - 1], xb_r.at[i, d - 1], at(xo(d), y, r, z))
            cp.start()
            xb[i, d] = cp
            sends.append(cp)

    def a_ring(i, s):
        if s == 1:
            for d in range(1, NX):
                xs[i, d].wait_recv()
        else:
            ring[i, 0, s - 1].wait_recv()
            ring[i, 1, s - 1].wait_recv()
        for way, sign in ((0, 1), (1, -1)):
            part = slice(None) if s < 4 else pl.ds(32 * way, 32)
            ref = wa.at[i, yo(-sign * (s - 1)), :, part, :]
            cp = copy(ref, ref, ya_s.at[i, way, s - 1], ya_r.at[i, way, s - 1], at(x, yo(sign), r, z))
            cp.start()
            ring[i, way, s] = cp
            sends.append(cp)

    lane = lax.broadcasted_iota(jnp.int32, (SUB, 128), 1) // 32

    def project(k):
        i = k // 2
        v = jnp.zeros((2 * TILE, 128), f32)
        q = jnp.zeros((2 * TILE, 128), f32)
        for j in range(4):
            if k % 2 == 0:
                w = jnp.concatenate([wa[i, 2 * j, 0:4].reshape(256, 128),
                                     wa[i, 2 * j + 1, 0:4].reshape(256, 128)], axis=0)
                p = wa[i, :, 4].reshape(512, 128)
            else:
                w = wb[i, j, 0:4].reshape(512, 128)
                p = wb[i, :, 4].reshape(512, 128)
            t = jnp.dot(tokbuf[:, j * 512:(j + 1) * 512], jnp.concatenate([w, p], axis=1),
                        preferred_element_type=f32)
            v = v + t[:, :128]
            q = q + jnp.where(lane == j, t[:, 128:], 0.0)
        q = q + pltpu.roll(q, 64, 1)
        q = q + pltpu.roll(q, 32, 1)
        for b in range(2):
            stage[k, b, 0:TILE, :] = v[b * TILE:(b + 1) * TILE].astype(bf16)
            rows = q[b * TILE:(b + 1) * TILE].reshape(4, PACK, 128)
            pk = rows[0]
            for j in range(1, 4):
                pk = jnp.where(lane[:PACK] == j, rows[j], pk)
            stage[k, b, TILE:, :] = pk.astype(bf16)

    tile_copies = {}

    def scatter(k):
        for b in range(2):
            cp = copy(stage.at[k, b], xr.at[z + 1], at_s.at[k, b], at_r.at[z], at(x, y, b, zo(dist(k))))
            tile_copies[k, b] = cp
            if k == 0 and b == 1:
                @pl.when(r == 0)
                def _():
                    cp.start()

                @pl.when(r == 1)
                def _():
                    xr[z + 1] = stage[0, 1]
            else:
                cp.start()

    a_small(0)
    b_small(0)
    a_small(1)
    b_small(1)
    a_ring(0, 1)
    b_large(0)
    a_small(2)
    b_small(2)
    a_ring(1, 1)
    b_large(1)
    a_ring(0, 2)
    a_ring(2, 1)
    b_large(2)
    a_ring(1, 2)
    a_ring(0, 3)
    a_ring(2, 2)
    a_ring(1, 3)
    a_ring(0, 4)
    tok_copy.wait_recv()

    def finish_b(i):
        for d in range(1, NX):
            xb[i, d].wait_recv()
        project(2 * i + 1)
        scatter(2 * i + 1)

    def finish_a(i):
        ring[i, 0, 4].wait_recv()
        ring[i, 1, 4].wait_recv()
        project(2 * i)
        scatter(2 * i)

    finish_b(0)
    a_ring(2, 3)
    finish_a(0)
    a_ring(1, 4)
    finish_b(1)
    a_ring(2, 4)
    finish_a(1)
    finish_b(2)
    finish_a(2)

    def await_tile(t):
        copy(stage.at[0, 0], xr.at[t + 1], at_s.at[0, 0], at_r.at[t], at(x, y, r, z)).wait_recv()

    last = NZ - 1

    def tile_in(t):
        @pl.when(jnp.logical_or(r == 0, z != t))
        def _():
            await_tile(t)

    tile_in(last)

    def halo(n):
        rows = pl.ds(112 + 32 * n, 16)
        return copy(xr.at[NZ, rows, :], xr.at[0, rows, :], h_s.at[n], h_r.at[n], (c + 1, z))

    @pl.when(c < 2 * NX * NY - 1)
    def _():
        halo(0).start()
        halo(1).start()

    for t in range(last):
        tile_in(t)

    @pl.when(c == 0)
    def _():
        xr[0, 112:128] = jnp.zeros((16, 128), bf16)
        xr[0, 144:160] = jnp.zeros((16, 128), bf16)

    @pl.when(c > 0)
    def _():
        for n in range(2):
            rows = pl.ds(112 + 32 * n, 16)
            copy(xr.at[NZ, rows, :], xr.at[0, rows, :], h_s.at[n], h_r.at[n], (c - 1, z)).wait_recv()

    ca = conv_ref[:, 0:128]
    cb = conv_ref[:, 128:160]
    cv = jnp.concatenate([ca[:, 32:], cb], axis=1)
    cqk = jnp.concatenate([ca[:, :32]] * 4, axis=1)
    plane = lax.broadcasted_iota(jnp.int32, (PACK, 128), 1)
    quad = 1.0 / (2.0 ** 0.5 * FEAT ** 0.5)
    one_row = jnp.where(lax.broadcasted_iota(jnp.int32, (8, 128), 0) == 0, 1.0, 0.0)

    def features(u, twice):
        parts = [u * u * quad]
        for d in range(1, 8):
            parts.append(u * pltpu.roll(u, FEAT - d, 0) * (quad * twice))
        parts.append((u * pltpu.roll(u, 8, 0) * (quad * twice))[:8])
        parts.append(u * FEAT ** -0.25)
        parts.append(one_row)
        return jnp.concatenate(parts, axis=0)

    @pl.loop(0, NZ)
    def _(t):
        before = xr[t, 112:128].astype(f32)
        now = xr[t + 1, 0:TILE].astype(f32)
        window = jnp.concatenate([before[8:], now], axis=0)
        acc = jnp.zeros((TILE, 128), f32)
        for o in range(4):
            acc = acc + cv[o:o + 1] * window[8 - o:8 - o + TILE]
        rows = pl.ds(pl.multiple_of(t * TILE, TILE), TILE)
        vb[rows, :] = acc.astype(bf16)
        pk = xr[t + 1, TILE:].astype(f32)
        before = xr[t, 144:160].astype(f32)
        edge = jnp.where(plane[:8] < 32, pltpu.roll(before[8:], 32, 1), pltpu.roll(pk[24:], 32, 1))
        window = jnp.concatenate([edge, pk], axis=0)
        qk = jnp.zeros((PACK, 128), f32)
        for o in range(4):
            qk = qk + cqk[o:o + 1] * window[8 - o:8 - o + PACK]
        wide = jnp.concatenate([qk] + [pltpu.roll(qk, 128 - 32 * j, 1) for j in range(1, 4)], axis=0)
        tall = wide.T
        fq[rows, :] = features(tall[0:FEAT], 2.0).T.astype(bf16)
        fk[t] = features(tall[FEAT:2 * FEAT], 1.0).astype(bf16)

    per = BLOCK // TILE
    ones = jnp.ones((8, BLOCK), bf16)
    for b in range(2):
        keys = jnp.concatenate([fk[b * per + t] for t in range(per)], axis=1)
        st[b] = jnp.dot(keys, vb[b * BLOCK:(b + 1) * BLOCK, :], preferred_element_type=f32)
        total = lax.dot_general(ones, keys, (((1,), (1,)), ((), ())), preferred_element_type=f32)
        st[b, TOT:TOT + 1, :] = total[0:1, 0:128]
        st[b, TOT + 1:TOT + 2, 0:32] = total[0:1, 128:160]
    loc[...] = st[0] + st[1]

    mine = pl.ds(pl.multiple_of(r * HALF, 8), HALF)
    other = pl.ds(pl.multiple_of((1 - r) * HALF, 8), HALF)
    partner = at(x, y, 1 - r, z)
    d1 = copy(loc.at[other, :], px, d1_s, d1_r, partner)
    d1.start()
    sends.append(d1)

    def within(b):
        for i in range(BLOCK // SUB):
            cols = (i + 1) * SUB
            keys = jnp.concatenate([fk[b * per + t] for t in range(cols // TILE)], axis=1)
            row = b * BLOCK + i * SUB
            w = jnp.dot(fq[row:row + SUB, :], keys, preferred_element_type=f32)
            causal = (lax.broadcasted_iota(jnp.int32, (SUB, cols), 0) + i * SUB
                      >= lax.broadcasted_iota(jnp.int32, (SUB, cols), 1))
            w = jnp.where(causal, w, 0.0)
            num[row:row + SUB, :] = jnp.dot(w.astype(bf16), vb[b * BLOCK:b * BLOCK + cols, :],
                                            preferred_element_type=f32)
            den[row:row + SUB, :] = jnp.broadcast_to(jnp.sum(w, axis=1, keepdims=True), (SUB, 128))

    d1.wait_recv()
    ch[...] = loc[mine, :] + px[...]
    sy = []
    for d in range(1, NY):
        cp = copy(ch, ybuf.at[d - 1], sy_s.at[d - 1], sy_r.at[d - 1], at(x, yo(d), r, z))
        cp.start()
        sy.append(cp)
    sends.extend(sy)
    within(0)
    within(1)
    total = ch[...]
    before = jnp.zeros((HALF, 128), f32)
    for d in range(1, NY):
        sy[d - 1].wait_recv()
        got = ybuf[d - 1]
        total = total + got
        before = before + jnp.where(y >= d, got, 0.0)
    tx[...] = total
    sx = []
    for d in range(1, NX):
        cp = copy(tx, xbuf.at[d - 1], sx_s.at[d - 1], sx_r.at[d - 1], at(xo(d), y, r, z))
        cp.start()
        sx.append(cp)
    sends.extend(sx)
    for d in range(1, NX):
        sx[d - 1].wait_recv()
        before = before + jnp.where(x >= d, xbuf[d - 1], 0.0)
    snd[...] = before + jnp.where(r == 0, loc[mine, :], 0.0)
    d2 = copy(snd, fin.at[mine, :], d2_s, d2_r, partner)
    d2.start()
    sends.append(d2)
    fin[mine, :] = before + jnp.where(r == 1, px[...], 0.0)
    d2.wait_recv()

    for b in range(2):
        state = fin[...] if b == 0 else fin[...] + st[0]
        high = state.astype(bf16)
        low = (state - high.astype(f32)).astype(bf16)
        row = jnp.concatenate([state[TOT:TOT + 1, :], state[TOT + 1:TOT + 2, 0:32]], axis=1)
        row_high = row.astype(bf16).astype(f32)
        which = lax.broadcasted_iota(jnp.int32, (16, PHI), 0)
        rows = jnp.where(which == 0, row_high, jnp.where(which == 1, row - row_high, 0.0)).astype(bf16)
        for i in range(BLOCK // SUB):
            at_rows = slice(b * BLOCK + i * SUB, b * BLOCK + (i + 1) * SUB)
            f = fq[at_rows, :]
            top = num[at_rows, :] + jnp.dot(f, high, preferred_element_type=f32)
            top = top + jnp.dot(f, low, preferred_element_type=f32)
            two = lax.dot_general(f, rows, (((1,), (1,)), ((), ())), preferred_element_type=f32)
            bottom = den[at_rows, :] + (two[:, 0:1] + two[:, 1:2])
            out_ref[at_rows, :] = (top / bottom).astype(bf16)

    @pl.when(r == 0)
    def _():
        z_copies[0].wait_send()
        tile_copies[0, 1].wait_send()

    for (k, b), cp in tile_copies.items():
        if (k, b) != (0, 1):
            cp.wait_send()
    for cp in sends:
        cp.wait_send()

    @pl.when(c < 2 * NX * NY - 1)
    def _():
        halo(0).wait_send()
        halo(1).wait_send()


def per_device(tokens, projection, conv_weight):
    vmem = pltpu.VMEM
    dma = pltpu.SemaphoreType.DMA
    return pl.pallas_call(
        kernel,
        out_shape=jax.ShapeDtypeStruct((ROWS, VW), bf16),
        in_specs=[pl.BlockSpec(memory_space=vmem)] * 3,
        out_specs=pl.BlockSpec(memory_space=vmem),
        scratch_shapes=[
            vmem((2 * TILE, D), bf16),
            vmem((5, 16, 128), bf16),
            vmem((5, 64, 128), bf16),
            vmem((3, NY, 5, 64, 128), bf16),
            vmem((3, NX, 5, 128, 128), bf16),
            vmem((6, 2, TILE + PACK, 128), bf16),
            vmem((NZ + 1, TILE + PACK, 128), bf16),
            vmem((ROWS, VW), bf16),
            vmem((ROWS, PHI), bf16),
            vmem((NZ, PHI, TILE), bf16),
            vmem((2, PHI, 128), f32),
            vmem((PHI, 128), f32),
            vmem((HALF, 128), f32),
            vmem((HALF, 128), f32),
            vmem((NY - 1, HALF, 128), f32),
            vmem((HALF, 128), f32),
            vmem((NX - 1, HALF, 128), f32),
            vmem((HALF, 128), f32),
            vmem((PHI, 128), f32),
            vmem((ROWS, 128), f32),
            vmem((ROWS, 128), f32),
            dma, dma,
            dma((6,)), dma((6,)),
            dma((3, NX - 1)), dma((3, NX - 1)),
            dma((3, 2, 4)), dma((3, 2, 4)),
            dma((3,)), dma((3,)),
            dma((3, NX - 1)), dma((3, NX - 1)),
            dma((6, 2)), dma((NZ,)),
            dma((2,)), dma((2,)),
            dma, dma,
            dma((NY - 1,)), dma((NY - 1,)),
            dma((NX - 1,)), dma((NX - 1,)),
            dma, dma,
        ],
        compiler_params=pltpu.CompilerParams(
            collective_id=0, has_side_effects=True, vmem_limit_bytes=48 * 2**20),
        name="fused",
    )(tokens, projection, conv_weight)


def solution(mesh):
    return jax.shard_map(
        per_device,
        mesh=mesh,
        in_specs=(P(("ctx", "tp"), None), P(None, "tp"), P(None, "tp")),
        out_specs=P("ctx", "tp"),
        check_vma=False,
    )
```

time: 416 us -> 99.7 us (0.24)
  waiting for transfers between devices: 351 us -> 0 us
  Pallas kernels: 0 us -> 97.3 us
  matrix products: 16 us -> 0 us
  other arithmetic: 15 us -> 0 us
  between operations: 14.1 us -> 0.03 us
  local copies, waits for them, and re-layouts: 15.2 us -> 2.22 us
    all_gather x2 -> x0, waiting for transfers between devices: 187 us -> none  [the longest x1 94.5 us: per_device(): lax.all_gather(tokens, 'tp', axis=0, tiled=True)]
    unnamed x4 -> x0, waiting for transfers between devices: 163 us -> none
    pallas_call x0 -> x1, Pallas kernels: none -> 97.3 us  [per_device(): pl.pallas_call(kernel, out_shape=jax.ShapeDtypeStruct((ROWS, VW), bf16),...]
    dot_general x14 -> x0, matrix products: 16 us -> none  [the longest x1 5 us: per_device(): jnp.dot(lax.all_gather(tokens, 'tp', axis=0, tiled=True), projection, pre...]
    reduce_sum x5 -> x0, other arithmetic: 6.18 us -> none  [the longest x1 4.67 us: per_device(): jnp.sum(jnp.where(earlier_mask[:, None, None], states, 0.0), axis=0)]
    concatenate x1 -> x0, other arithmetic: 4.85 us -> none  [taylor(): jnp.concatenate([ones_col, linear, quadratic], axis=1).astype(jnp.bfloat16)]
    unnamed x28 -> x6, local copies, waits for them, and re-layouts: 6.98 us -> 2.22 us
  transfers between devices with their start and end apart: 4 -> 0, of which waited for: 3 -> 0; matrix products, arithmetic and copies ran while one was open for 7% -> 0% of each run, Pallas kernels for 0% -> 0%
where the time goes in v1:
time: 99.7 us; the launch traced here: 99.6 us
  Pallas kernels  97.3 us (98%)
  local copies, waits for them, and re-layouts  2.22 us (2%)
    pallas_call x1, Pallas kernels, per_device(): pl.pallas_call(kernel, out_shape=jax.ShapeDtypeStruct((ROWS, VW), bf16),...  97.3 us
    unnamed x6, local copies, waits for them, and re-layouts  2.22 us

profile of v1, /device:TPU:1, one launch (start us, length us, event | category | flops | bytes accessed | tf_op | source)
XLA Modules:
  0.0 99.6 jit_solution(10132670491981429808)
XLA Ops:
  0.0 0.0 copy-start.1
  0.0 0.0 copy-start
  0.0 1.5 %copy.4.proj_ref = bf16[2048,160]{1,0:T(8,128)(2,1)S(1)} copy(bf16[2048,160]{0,1:T(8,128)(2,1)} %param.4) | data formatting | bytes 1310720 | tf_op args[1]
  1.5 0.0 copy-done.1
  1.5 0.0 copy-done
  1.5 97.3 %fused.1 = bf16[1536,128]{1,0:T(8,128)(2,1)S(1)} custom-call(bf16[128,2048]{1,0:T(8,128)(2,1)S(1)} %copy-done, bf16[2048,160]{1,0:T(8,128)(2,1)S(1)} %copy.4.proj_ref, f32[4,160]{1,0:T(4,128)S(1)} %copy-done.1), custom_call_target="tpu_custom_call" | custom-call | tf_op jit(solution)/shard_map/fused/pallas_call | solution.py:435
  98.8 0.7 copy.6
Async XLA Ops:
  0.0 1.5 %copy-start.1 = (f32[4,160]{1,0:T(4,128)S(1)}, f32[4,160]{1,0:T(4,128)}, u32[]{:S(2)}) copy-start(f32[4,160]{1,0:T(4,128)} %conv_ref.1) | copy-start | bytes 7684
  0.0 1.5 %copy-start = (bf16[128,2048]{1,0:T(8,128)(2,1)S(1)}, bf16[128,2048]{1,0:T(8,128)(2,1)}, u32[]{:S(2)}) copy-start(bf16[128,2048]{1,0:T(8,128)(2,1)} %tok_ref.1) | copy-start | bytes 1572868

commit v2 on v1

v2 whole, which is shorter than its diff:
```python
import jax
import jax.numpy as jnp
from jax import lax
from jax.experimental import pallas as pl
from jax.experimental.pallas import tpu as pltpu
from jax.sharding import PartitionSpec as P

NX, NY, NZ = 4, 8, 12
D = 2048
FEAT = 16
VW = 128
WIDTH = 2 * FEAT + VW
TILE = 128
ROWS = TILE * NZ
PHI = 160
HALF = PHI // 2
TOT = 153
BLOCK = 768
SUB = 256
MESH = pl.DeviceIdType.MESH
bf16, f32 = jnp.bfloat16, jnp.float32


def dot_nt(a, b):
    return lax.dot_general(a, b, (((1,), (1,)), ((), ())), preferred_element_type=f32)


def kernel(tok_ref, proj_ref, conv_ref, out_ref,
           tokbuf, wr, wx, stage, xr, cw, vt, fq, fk, st, loc, px, ch, ybuf, tx, xbuf, snd, fin, num, den,
           tk_s, tk_r, zr_s, zr_r, zx_s, zx_r, xs_s, xs_r, ya_s, ya_r, yb_s, yb_r, xb_s, xb_r, at_s, at_r, h_s, h_r,
           d1_s, d1_r, sy_s, sy_r, sx_s, sx_r, d2_s, d2_r):
    c = lax.axis_index("ctx")
    z = lax.axis_index("tp")
    r = lax.rem(c, 2)
    y = lax.rem(c // 2, NY)
    x = c // (2 * NY)
    xpar = lax.rem(x, 2)
    ypar = lax.rem(y, 2)
    zpar = lax.rem(z, 2)

    def at(xx, yy, rr, zz):
        return ((xx * NY + yy) * 2 + rr, zz)

    def xo(d):
        return lax.rem(x + d + NX, NX)

    def yo(d):
        return lax.rem(y + d + NY, NY)

    def zo(d):
        return lax.rem(z + d + NZ, NZ)

    def copy(src, dst, ss, rs, dev):
        return pltpu.make_async_remote_copy(
            src_ref=src, dst_ref=dst, send_sem=ss, recv_sem=rs, device_id=dev, device_id_type=MESH)

    barrier = pltpu.get_barrier_semaphore()

    def greet(dev):
        pl.semaphore_signal(barrier, inc=1, device_id=dev, device_id_type=MESH)

    greet(at(x, y, 1 - r, z))
    for d in range(1, NX):
        greet(at(xo(d), y, r, z))
    for d in range(1, NY):
        greet(at(x, yo(d), r, z))
    for d in range(1, NZ):
        greet(at(x, y, r, zo(d)))
        greet(at(x, y, 1 - r, zo(d)))

    @pl.when(jnp.logical_and(r == 0, c > 0))
    def _():
        greet((c - 1, z))

    tokbuf[zpar * 2 + r] = tok_ref[...]
    ca = conv_ref[...]
    ca = jnp.concatenate([ca, ca], axis=0)
    taps_qk = ca[:, 0:128].T
    taps_v = ca[:, 32:WIDTH].T
    for o in range(4):
        cw[o, 0:32] = jnp.broadcast_to(taps_qk[0:32, o:o + 1], (32, 128))
        cw[o, 32:] = jnp.broadcast_to(taps_v[:, o:o + 1], (VW, 128))

    pl.semaphore_wait(barrier, NX + NY - 1 + 2 * (NZ - 1) + r * (1 - c // (2 * NX * NY - 1)))

    way_z = 2 * zpar - 1
    sends = []

    def guard(i, body):
        if i == 2:
            pl.when(r == 0)(body)
        else:
            body()

    def dist(i):
        return 5 - r - 2 * i

    zpair = z - way_z
    partner = at(x, y, 1 - r, z)
    own_tok = tokbuf.at[zpar * 2 + r]
    far_tok = tokbuf.at[(1 - zpar) * 2 + r]
    tok_near = copy(tok_ref, own_tok, tk_s.at[0], tk_r.at[0], partner)
    tok_pair = copy(tok_ref, own_tok, tk_s.at[1], tk_r.at[1], at(x, y, r, zpair))
    tok_relay = copy(far_tok, far_tok, tk_s.at[2], tk_r.at[2], partner)

    rhalf = pl.ds(pl.multiple_of(xpar * 80, 16), 80)
    xhalf = pl.ds(pl.multiple_of(ypar * 128, 128), 128)
    rpiece = proj_ref.at[rhalf, pl.ds(pl.multiple_of(y * 128, 128), 128)]
    xpiece = proj_ref.at[:, pl.ds(pl.multiple_of(1024 + x * 256 + ypar * 128, 128), 128)]
    zr, zx, xs, yb, ring, xb = {}, {}, {}, {}, {}, {}
    for i in range(3):
        d = dist(i)
        to = at(x, y, r, zo(d * (1 - 2 * lax.rem(z + d, 2))))
        zr[i] = copy(rpiece, wr.at[i, y, rhalf, :], zr_s.at[i], zr_r.at[i], to)
        zx[i] = copy(xpiece, wx.at[i, x, :, xhalf], zx_s.at[i], zx_r.at[i], to)
        ref = wr.at[i, y, rhalf, :]
        xs[i] = copy(ref, ref, xs_s.at[i], xs_r.at[i], at(x + 1 - 2 * xpar, y, r, z))
        ref = wx.at[i, x, :, xhalf]
        yb[i] = copy(ref, ref, yb_s.at[i], yb_r.at[i], at(x, y + 1 - 2 * ypar, r, z))
        for dx in range(1, NX):
            ref = wx.at[i, x]
            xb[i, dx] = copy(ref, ref, xb_s.at[i, dx - 1], xb_r.at[i, dx - 1], at(xo(dx), y, r, z))
        for s in range(1, 5):
            for way, sign in ((0, 1), (1, -1)):
                ref = wr.at[i, yo(-sign * (s - 1))]
                if s == 4:
                    ref = wr.at[i, yo(-sign * 3), pl.ds(80 * way, 80), :]
                ring[i, way, s] = copy(ref, ref, ya_s.at[i, way, s - 1], ya_r.at[i, way, s - 1], at(x, yo(sign), r, z))

    def z_start(i):
        zr[i].start()
        zx[i].start()

    def small(i):
        zr[i].wait_recv()
        xs[i].start()
        zx[i].wait_recv()
        yb[i].start()

    def first(i):
        xs[i].wait_recv()
        ring[i, 0, 1].start()
        ring[i, 1, 1].start()
        yb[i].wait_recv()
        for dx in range(1, NX):
            xb[i, dx].start()

    def step(i, s):
        for way in range(2):
            ring[i, way, s - 1].wait_recv()
            ring[i, way, s].start()

    def gathered(i):
        for dx in range(1, NX):
            xb[i, dx].wait_recv()
        for way in range(2):
            ring[i, way, 4].wait_recv()

    def project(i, block):
        acc = jnp.zeros((WIDTH, 4 * TILE), f32)
        for j in range(8):
            acc = acc + dot_nt(block(j), tokbuf[:, :, j * 256:(j + 1) * 256].reshape(4 * TILE, 256))
        for s in range(4):
            stage[i, s] = acc[:, s * TILE:(s + 1) * TILE].astype(bf16)

    def from_gather(i):
        def block(j):
            if j < 4:
                return jnp.concatenate([wr[i, 2 * j], wr[i, 2 * j + 1]], axis=1)
            return wx[i, j - 4]
        return block

    def from_own(j):
        return proj_ref[:, j * 256:(j + 1) * 256]

    tiles = {}
    for i in range(3):
        for s in range(4):
            source = 2 * (z // 2) + s // 2
            tiles[i, s] = copy(stage.at[i, s], xr.at[source + 1], at_s.at[i, s], at_r.at[source],
                               at(x, y, s % 2, zo(way_z * dist(i))))

    slots = range(3)
    for i in slots:
        guard(i, lambda i=i: z_start(i))
    tok_pair.start()
    tok_near.start()
    for i in slots:
        guard(i, lambda i=i: small(i))
    for i in slots:
        guard(i, lambda i=i: first(i))
    for i in slots:
        guard(i, lambda i=i: step(i, 2))
    tok_near.wait_recv()
    for i in slots:
        guard(i, lambda i=i: step(i, 3))
    tok_pair.wait_recv()
    tok_relay.start()
    for i in slots:
        guard(i, lambda i=i: step(i, 4))
    tok_relay.wait_recv()
    for i in range(2):
        gathered(i)
        project(i, from_gather(i))
        for s in range(4):
            tiles[i, s].start()

    @pl.when(r == 0)
    def _():
        gathered(2)
        project(2, from_gather(2))
        for s in range(4):
            tiles[2, s].start()

    @pl.when(r == 1)
    def _():
        project(2, from_own)
        for s in range(4):
            if s % 2 == 0:
                tiles[2, s].start()
            else:
                xr[2 * (z // 2) + s // 2 + 1] = stage[2, s]

    last = NZ - 1

    def tile_in(t):
        @pl.when(jnp.logical_or(r == 0, z // 2 != t // 2))
        def _():
            copy(stage.at[0, 0], xr.at[t + 1], at_s.at[0, 0], at_r.at[t], partner).wait_recv()

    def halo(dev):
        return copy(xr.at[NZ], xr.at[0], h_s, h_r, (dev, z))

    tile_in(last)

    @pl.when(c < 2 * NX * NY - 1)
    def _():
        halo(c + 1).start()

    for t in range(last):
        tile_in(t)

    @pl.when(c == 0)
    def _():
        xr[0] = jnp.zeros((WIDTH, TILE), bf16)

    @pl.when(c > 0)
    def _():
        halo(c - 1).wait_recv()

    lane = lax.broadcasted_iota(jnp.int32, (WIDTH, TILE), 1)
    quad = 1.0 / (2.0 ** 0.5 * FEAT ** 0.5)
    one_row = jnp.where(lax.broadcasted_iota(jnp.int32, (8, TILE), 0) == 0, 1.0, 0.0)

    def features(u, twice):
        parts = [u * u * quad]
        for d in range(1, 8):
            parts.append(u * pltpu.roll(u, FEAT - d, 0) * (quad * twice))
        parts.append((u * pltpu.roll(u, 8, 0) * (quad * twice))[:8])
        parts.append(u * FEAT ** -0.25)
        parts.append(one_row)
        return jnp.concatenate(parts, axis=0)

    @pl.loop(0, NZ)
    def _(t):
        before = xr[t].astype(f32)
        now = xr[t + 1].astype(f32)
        acc = cw[0] * now
        for o in range(1, 4):
            acc = acc + cw[o] * pltpu.roll(jnp.where(lane >= TILE - o, before, now), o, 1)
        vt[t] = acc[2 * FEAT:].astype(bf16)
        rows = pl.ds(pl.multiple_of(t * TILE, TILE), TILE)
        fq[rows, :] = features(acc[0:FEAT], 2.0).T.astype(bf16)
        fk[t] = features(acc[FEAT:2 * FEAT], 1.0).astype(bf16)

    per = BLOCK // TILE

    def lanes(ref, b, n):
        return jnp.concatenate([ref[b * per + t] for t in range(n)], axis=1)

    ones = jnp.ones((8, BLOCK), bf16)
    for b in range(2):
        keys = lanes(fk, b, per)
        st[b] = dot_nt(keys, lanes(vt, b, per))
        total = dot_nt(ones, keys)
        st[b, TOT:TOT + 1, :] = total[0:1, 0:128]
        st[b, TOT + 1:TOT + 2, 0:32] = total[0:1, 128:160]
    loc[...] = st[0] + st[1]

    mine = pl.ds(pl.multiple_of(r * HALF, 8), HALF)
    other = pl.ds(pl.multiple_of((1 - r) * HALF, 8), HALF)
    d1 = copy(loc.at[other, :], px, d1_s, d1_r, partner)
    d1.start()
    sends.append(d1)

    def within(b):
        for i in range(BLOCK // SUB):
            cols = (i + 1) * SUB
            keys = lanes(fk, b, cols // TILE)
            row = b * BLOCK + i * SUB
            w = jnp.dot(fq[row:row + SUB, :], keys, preferred_element_type=f32)
            causal = (lax.broadcasted_iota(jnp.int32, (SUB, cols), 0) + i * SUB
                      >= lax.broadcasted_iota(jnp.int32, (SUB, cols), 1))
            w = jnp.where(causal, w, 0.0)
            num[row:row + SUB, :] = dot_nt(w.astype(bf16), lanes(vt, b, cols // TILE))
            den[row:row + SUB, :] = jnp.broadcast_to(jnp.sum(w, axis=1, keepdims=True), (SUB, 128))

    d1.wait_recv()
    ch[...] = loc[mine, :] + px[...]
    sy = []
    for d in range(1, NY):
        cp = copy(ch, ybuf.at[d - 1], sy_s.at[d - 1], sy_r.at[d - 1], at(x, yo(d), r, z))
        cp.start()
        sy.append(cp)
    sends.extend(sy)
    within(0)
    within(1)
    total = ch[...]
    before = jnp.zeros((HALF, 128), f32)
    for d in range(1, NY):
        sy[d - 1].wait_recv()
        got = ybuf[d - 1]
        total = total + got
        before = before + jnp.where(y >= d, got, 0.0)
    tx[...] = total
    sx = []
    for d in range(1, NX):
        cp = copy(tx, xbuf.at[d - 1], sx_s.at[d - 1], sx_r.at[d - 1], at(xo(d), y, r, z))
        cp.start()
        sx.append(cp)
    sends.extend(sx)
    for d in range(1, NX):
        sx[d - 1].wait_recv()
        before = before + jnp.where(x >= d, xbuf[d - 1], 0.0)
    snd[...] = before + jnp.where(r == 0, loc[mine, :], 0.0)
    d2 = copy(snd, fin.at[mine, :], d2_s, d2_r, partner)
    d2.start()
    sends.append(d2)
    fin[mine, :] = before + jnp.where(r == 1, px[...], 0.0)
    d2.wait_recv()

    for b in range(2):
        state = fin[...] if b == 0 else fin[...] + st[0]
        high = state.astype(bf16)
        low = (state - high.astype(f32)).astype(bf16)
        row = jnp.concatenate([state[TOT:TOT + 1, :], state[TOT + 1:TOT + 2, 0:32]], axis=1)
        row_high = row.astype(bf16).astype(f32)
        which = lax.broadcasted_iota(jnp.int32, (16, PHI), 0)
        rows = jnp.where(which == 0, row_high, jnp.where(which == 1, row - row_high, 0.0)).astype(bf16)
        for i in range(BLOCK // SUB):
            at_rows = slice(b * BLOCK + i * SUB, b * BLOCK + (i + 1) * SUB)
            f = fq[at_rows, :]
            top = num[at_rows, :] + jnp.dot(f, high, preferred_element_type=f32)
            top = top + jnp.dot(f, low, preferred_element_type=f32)
            two = dot_nt(f, rows)
            bottom = den[at_rows, :] + (two[:, 0:1] + two[:, 1:2])
            out_ref[at_rows, :] = (top / bottom).astype(bf16)

    def left(i):
        zr[i].wait_send()
        zx[i].wait_send()
        xs[i].wait_send()
        yb[i].wait_send()
        for dx in range(1, NX):
            xb[i, dx].wait_send()
        for way in range(2):
            for s in range(1, 5):
                ring[i, way, s].wait_send()
        for s in range(1, 4, 2):
            tiles[i, s].wait_send()

    for i in range(3):
        guard(i, lambda i=i: left(i))
        for s in range(0, 4, 2):
            tiles[i, s].wait_send()
    for cp in (tok_near, tok_pair, tok_relay):
        cp.wait_send()
    for cp in sends:
        cp.wait_send()

    @pl.when(c < 2 * NX * NY - 1)
    def _():
        halo(c + 1).wait_send()


def per_device(tokens, projection, conv_weight):
    vmem = pltpu.VMEM
    dma = pltpu.SemaphoreType.DMA
    return pl.pallas_call(
        kernel,
        out_shape=jax.ShapeDtypeStruct((ROWS, VW), bf16),
        in_specs=[pl.BlockSpec(memory_space=vmem)] * 3,
        out_specs=pl.BlockSpec(memory_space=vmem),
        scratch_shapes=[
            vmem((4, TILE, D), bf16),
            vmem((3, NY, WIDTH, 128), bf16),
            vmem((3, NX, WIDTH, 256), bf16),
            vmem((3, 4, WIDTH, TILE), bf16),
            vmem((NZ + 1, WIDTH, TILE), bf16),
            vmem((4, WIDTH, TILE), f32),
            vmem((NZ, VW, TILE), bf16),
            vmem((ROWS, PHI), bf16),
            vmem((NZ, PHI, TILE), bf16),
            vmem((2, PHI, 128), f32),
            vmem((PHI, 128), f32),
            vmem((HALF, 128), f32),
            vmem((HALF, 128), f32),
            vmem((NY - 1, HALF, 128), f32),
            vmem((HALF, 128), f32),
            vmem((NX - 1, HALF, 128), f32),
            vmem((HALF, 128), f32),
            vmem((PHI, 128), f32),
            vmem((ROWS, 128), f32),
            vmem((ROWS, 128), f32),
            dma((3,)), dma((3,)),
            dma((3,)), dma((3,)),
            dma((3,)), dma((3,)),
            dma((3,)), dma((3,)),
            dma((3, 2, 4)), dma((3, 2, 4)),
            dma((3,)), dma((3,)),
            dma((3, NX - 1)), dma((3, NX - 1)),
            dma((3, 4)), dma((NZ,)),
            dma, dma,
            dma, dma,
            dma((NY - 1,)), dma((NY - 1,)),
            dma((NX - 1,)), dma((NX - 1,)),
            dma, dma,
        ],
        compiler_params=pltpu.CompilerParams(
            collective_id=0, has_side_effects=True, vmem_limit_bytes=48 * 2**20),
        name="fused",
    )(tokens, projection.T, conv_weight)


def solution(mesh):
    return jax.shard_map(
        per_device,
        mesh=mesh,
        in_specs=(P(("ctx", "tp"), None), P(None, "tp"), P(None, "tp")),
        out_specs=P("ctx", "tp"),
        check_vma=False,
    )
```

time: 99.7 us -> 86.7 us (0.87)
  Pallas kernels: 97.3 us -> 82.9 us
  local copies, waits for them, and re-layouts: 2.22 us -> 3.56 us
    pallas_call x1, Pallas kernels: 97.3 us -> 82.9 us  [per_device(): pl.pallas_call(kernel, out_shape=jax.ShapeDtypeStruct((ROWS, VW), bf16),...]
    unnamed x6 -> x7, local copies, waits for them, and re-layouts: 2.22 us -> 3.56 us
where the time goes in v2:
time: 86.7 us; the launch traced here: 86.5 us
  Pallas kernels  82.9 us (96%)
  local copies, waits for them, and re-layouts  3.56 us (4%)
    pallas_call x1, Pallas kernels, per_device(): pl.pallas_call(kernel, out_shape=jax.ShapeDtypeStruct((ROWS, VW), bf16),...  82.9 us
    unnamed x7, local copies, waits for them, and re-layouts  3.56 us

profile of v2, /device:TPU:1, one launch (start us, length us, event | category | flops | bytes accessed | tf_op | source)
XLA Modules:
  0.0 86.5 jit_solution(950424502091414006)
XLA Ops:
  0.0 0.0 copy-start
  0.0 1.1 %copy-done = bf16[2048,160]{0,1:T(8,128)(2,1)S(1)} copy-done((bf16[2048,160]{0,1:T(8,128)(2,1)S(1)}, bf16[2048,160]{0,1:T(8,128)(2,1)}, u32[]{:S(2)}) %copy-start) | copy-done | bytes 655384
  1.1 0.0 copy-start.1
  1.1 1.0 %copy-done.1 = bf16[128,2048]{1,0:T(8,128)(2,1)S(1)} copy-done((bf16[128,2048]{1,0:T(8,128)(2,1)S(1)}, bf16[128,2048]{1,0:T(8,128)(2,1)}, u32[]{:S(2)}) %copy-start.1) | copy-done | bytes 524312
  2.1 0.0 copy-start.2
  2.1 0.7 copy-done.2
  2.8 82.9 %fused.1 = bf16[1536,128]{1,0:T(8,128)(2,1)S(1)} custom-call(bf16[128,2048]{1,0:T(8,128)(2,1)S(1)} %copy-done.1, bf16[160,2048]{1,0:T(8,128)(2,1)S(1)} %bitcast.1, f32[4,160]{1,0:T(4,128)S(1)} %copy-done.2), custom_call_target="tpu_custom_call" | custom-call | tf_op jit(solution)/shard_map/fused/pallas_call | solution.py:389
  85.7 0.7 copy.5
Async XLA Ops:
  0.0 1.1 %copy-start = (bf16[2048,160]{0,1:T(8,128)(2,1)S(1)}, bf16[2048,160]{0,1:T(8,128)(2,1)}, u32[]{:S(2)}) copy-start(bf16[2048,160]{0,1:T(8,128)(2,1)} %param.4) | copy-start | bytes 1966084
  1.1 1.0 %copy-start.1 = (bf16[128,2048]{1,0:T(8,128)(2,1)S(1)}, bf16[128,2048]{1,0:T(8,128)(2,1)}, u32[]{:S(2)}) copy-start(bf16[128,2048]{1,0:T(8,128)(2,1)} %tok_ref.1) | copy-start | bytes 1572868
  2.1 0.7 copy-start.2

commit v3 on v2

--- a/solution.py
+++ b/solution.py
@@ -14,6 +14,7 @@
 ROWS = TILE * NZ
 PHI = 160
 HALF = PHI // 2
+PART = HALF // 2
 TOT = 153
 BLOCK = 768
 SUB = 256
@@ -26,7 +27,7 @@
 
 
 def kernel(tok_ref, proj_ref, conv_ref, out_ref,
-           tokbuf, wr, wx, stage, xr, cw, vt, fq, fk, st, loc, px, ch, ybuf, tx, xbuf, snd, fin, num, den,
+           tokbuf, wr, wx, stage, xr, cw, vt, fq, fk, st, loc, px, ch, ybuf, tx, xbuf, pb, snd, fin, num, den,
            tk_s, tk_r, zr_s, zr_r, zx_s, zx_r, xs_s, xs_r, ya_s, ya_r, yb_s, yb_r, xb_s, xb_r, at_s, at_r, h_s, h_r,
            d1_s, d1_r, sy_s, sy_r, sx_s, sx_r, d2_s, d2_r):
     c = lax.axis_index("ctx")
@@ -156,12 +157,13 @@
         for way in range(2):
             ring[i, way, 4].wait_recv()
 
-    def project(i, block):
-        acc = jnp.zeros((WIDTH, 4 * TILE), f32)
+    def project(i, half, block):
+        first_set = 2 * (zpar if half == 0 else 1 - zpar)
+        acc = jnp.zeros((WIDTH, 2 * TILE), f32)
         for j in range(8):
-            acc = acc + dot_nt(block(j), tokbuf[:, :, j * 256:(j + 1) * 256].reshape(4 * TILE, 256))
-        for s in range(4):
-            stage[i, s] = acc[:, s * TILE:(s + 1) * TILE].astype(bf16)
+            acc = acc + dot_nt(block(j), tokbuf[pl.ds(first_set, 2), :, j * 256:(j + 1) * 256].reshape(2 * TILE, 256))
+        for q in range(2):
+            stage[i, 2 * half + q] = acc[:, q * TILE:(q + 1) * TILE].astype(bf16)
 
     def from_gather(i):
         def block(j):
@@ -175,51 +177,62 @@
 
     tiles = {}
     for i in range(3):
-        for s in range(4):
-            source = 2 * (z // 2) + s // 2
-            tiles[i, s] = copy(stage.at[i, s], xr.at[source + 1], at_s.at[i, s], at_r.at[source],
-                               at(x, y, s % 2, zo(way_z * dist(i))))
+        for half, plane in ((0, z), (1, zpair)):
+            for q in range(2):
+                tiles[i, half, q] = copy(stage.at[i, 2 * half + q], xr.at[plane + 1], at_s.at[i, 2 * half + q],
+                                         at_r.at[plane], at(x, y, q, zo(way_z * dist(i))))
+
+    def work(i, half):
+        project(i, half, from_gather(i))
+        for q in range(2):
+            tiles[i, half, q].start()
+
+    def work_own(half, plane):
+        project(2, half, from_own)
+        tiles[2, half, 0].start()
+        xr[plane + 1] = stage[2, 2 * half + 1]
 
     slots = range(3)
     for i in slots:
         guard(i, lambda i=i: z_start(i))
+    tok_near.start()
+    small(0)
     tok_pair.start()
-    tok_near.start()
-    for i in slots:
-        guard(i, lambda i=i: small(i))
+    small(1)
+    guard(2, lambda: small(2))
     for i in slots:
         guard(i, lambda i=i: first(i))
-    for i in slots:
-        guard(i, lambda i=i: step(i, 2))
+    for n in range(2, 5):
+        for i in slots:
+            guard(i, lambda i=i: step(i, n))
     tok_near.wait_recv()
-    for i in slots:
-        guard(i, lambda i=i: step(i, 3))
+    for i in range(2):
+        gathered(i)
+        work(i, 0)
+
+    @pl.when(r == 0)
+    def _():
+        gathered(2)
+        work(2, 0)
+
     tok_pair.wait_recv()
     tok_relay.start()
-    for i in slots:
-        guard(i, lambda i=i: step(i, 4))
+
+    @pl.when(r == 1)
+    def _():
+        work_own(0, z)
+
     tok_relay.wait_recv()
     for i in range(2):
-        gathered(i)
-        project(i, from_gather(i))
-        for s in range(4):
-            tiles[i, s].start()
+        work(i, 1)
 
     @pl.when(r == 0)
     def _():
-        gathered(2)
-        project(2, from_gather(2))
-        for s in range(4):
-            tiles[2, s].start()
+        work(2, 1)
 
     @pl.when(r == 1)
     def _():
-        project(2, from_own)
-        for s in range(4):
-            if s % 2 == 0:
-                tiles[2, s].start()
-            else:
-                xr[2 * (z // 2) + s // 2 + 1] = stage[2, s]
+        work_own(1, zpair)
 
     last = NZ - 1
 
@@ -239,14 +252,6 @@
 
     for t in range(last):
         tile_in(t)
-
-    @pl.when(c == 0)
-    def _():
-        xr[0] = jnp.zeros((WIDTH, TILE), bf16)
-
-    @pl.when(c > 0)
-    def _():
-        halo(c - 1).wait_recv()
 
     lane = lax.broadcasted_iota(jnp.int32, (WIDTH, TILE), 1)
     quad = 1.0 / (2.0 ** 0.5 * FEAT ** 0.5)
@@ -261,17 +266,30 @@
         parts.append(one_row)
         return jnp.concatenate(parts, axis=0)
 
-    @pl.loop(0, NZ)
-    def _(t):
+    def convolve(t):
         before = xr[t].astype(f32)
         now = xr[t + 1].astype(f32)
         acc = cw[0] * now
         for o in range(1, 4):
             acc = acc + cw[o] * pltpu.roll(jnp.where(lane >= TILE - o, before, now), o, 1)
         vt[t] = acc[2 * FEAT:].astype(bf16)
-        rows = pl.ds(pl.multiple_of(t * TILE, TILE), TILE)
+        rows = pl.ds(t * TILE if isinstance(t, int) else pl.multiple_of(t * TILE, TILE), TILE)
         fq[rows, :] = features(acc[0:FEAT], 2.0).T.astype(bf16)
         fk[t] = features(acc[FEAT:2 * FEAT], 1.0).astype(bf16)
+
+    @pl.loop(1, NZ)
+    def _(t):
+        convolve(t)
+
+    @pl.when(c == 0)
+    def _():
+        xr[0] = jnp.zeros((WIDTH, TILE), bf16)
+
+    @pl.when(c > 0)
+    def _():
+        halo(c - 1).wait_recv()
+
+    convolve(0)
 
     per = BLOCK // TILE
 
@@ -306,32 +324,55 @@
             den[row:row + SUB, :] = jnp.broadcast_to(jnp.sum(w, axis=1, keepdims=True), (SUB, 128))
 
     d1.wait_recv()
-    ch[...] = loc[mine, :] + px[...]
-    sy = []
+    chip = loc[mine, :] + px[...]
+    ch[0] = chip[:PART]
+    ch[1] = chip[PART:]
+
+    def to_y(src, dst, ss, rs):
+        out = []
+        for d in range(1, NY):
+            cp = copy(src(d), dst.at[d - 1], ss.at[d - 1], rs.at[d - 1], at(x, yo(d), r, z))
+            cp.start()
+            out.append(cp)
+        sends.extend(out)
+        return out
+
+    def to_x(src, dst, ss, rs):
+        out = []
+        for d in range(1, NX):
+            cp = copy(src, dst.at[d - 1], ss.at[d - 1], rs.at[d - 1], at(xo(d), y, r, z))
+            cp.start()
+            out.append(cp)
+        sends.extend(out)
+        return out
+
+    x_second = to_x(ch.at[1], xbuf.at[1], sx_s.at[1], sx_r.at[1])
+    y_first = to_y(lambda d: ch.at[0], ybuf.at[0], sy_s.at[0], sy_r.at[0])
+    within(0)
+    second = jnp.zeros((PART, 128), f32)
+    for d in range(1, NX):
+        x_second[d - 1].wait_recv()
+        second = second + jnp.where(x >= d, xbuf[1, d - 1], 0.0)
+    pb[0] = second
+    pb[1] = second + ch[1]
+    y_second = to_y(lambda d: pb.at[1 - (y + d) // NY], ybuf.at[1], sy_s.at[1], sy_r.at[1])
+    within(1)
+    total = ch[0]
+    first_rows = jnp.zeros((PART, 128), f32)
     for d in range(1, NY):
-        cp = copy(ch, ybuf.at[d - 1], sy_s.at[d - 1], sy_r.at[d - 1], at(x, yo(d), r, z))
-        cp.start()
-        sy.append(cp)
-    sends.extend(sy)
-    within(0)
-    within(1)
-    total = ch[...]
-    before = jnp.zeros((HALF, 128), f32)
+        y_first[d - 1].wait_recv()
+        got = ybuf[0, d - 1]
+        total = total + got
+        first_rows = first_rows + jnp.where(y >= d, got, 0.0)
+    tx[...] = total
+    x_first = to_x(tx, xbuf.at[0], sx_s.at[0], sx_r.at[0])
     for d in range(1, NY):
-        sy[d - 1].wait_recv()
-        got = ybuf[d - 1]
-        total = total + got
-        before = before + jnp.where(y >= d, got, 0.0)
-    tx[...] = total
-    sx = []
+        y_second[d - 1].wait_recv()
+        second = second + ybuf[1, d - 1]
     for d in range(1, NX):
-        cp = copy(tx, xbuf.at[d - 1], sx_s.at[d - 1], sx_r.at[d - 1], at(xo(d), y, r, z))
-        cp.start()
-        sx.append(cp)
-    sends.extend(sx)
-    for d in range(1, NX):
-        sx[d - 1].wait_recv()
-        before = before + jnp.where(x >= d, xbuf[d - 1], 0.0)
+        x_first[d - 1].wait_recv()
+        first_rows = first_rows + jnp.where(x >= d, xbuf[0, d - 1], 0.0)
+    before = jnp.concatenate([first_rows, second], axis=0)
     snd[...] = before + jnp.where(r == 0, loc[mine, :], 0.0)
     d2 = copy(snd, fin.at[mine, :], d2_s, d2_r, partner)
     d2.start()
@@ -366,13 +407,13 @@
         for way in range(2):
             for s in range(1, 5):
                 ring[i, way, s].wait_send()
-        for s in range(1, 4, 2):
-            tiles[i, s].wait_send()
+        for half in range(2):
+            tiles[i, half, 1].wait_send()
 
     for i in range(3):
         guard(i, lambda i=i: left(i))
-        for s in range(0, 4, 2):
-            tiles[i, s].wait_send()
+        for half in range(2):
+            tiles[i, half, 0].wait_send()
     for cp in (tok_near, tok_pair, tok_relay):
         cp.wait_send()
     for cp in sends:
@@ -404,10 +445,11 @@
             vmem((2, PHI, 128), f32),
             vmem((PHI, 128), f32),
             vmem((HALF, 128), f32),
-            vmem((HALF, 128), f32),
-            vmem((NY - 1, HALF, 128), f32),
-            vmem((HALF, 128), f32),
-            vmem((NX - 1, HALF, 128), f32),
+            vmem((2, PART, 128), f32),
+            vmem((2, NY - 1, PART, 128), f32),
+            vmem((PART, 128), f32),
+            vmem((2, NX - 1, PART, 128), f32),
+            vmem((2, PART, 128), f32),
             vmem((HALF, 128), f32),
             vmem((PHI, 128), f32),
             vmem((ROWS, 128), f32),
@@ -422,8 +464,8 @@
             dma((3, 4)), dma((NZ,)),
             dma, dma,
             dma, dma,
-            dma((NY - 1,)), dma((NY - 1,)),
-            dma((NX - 1,)), dma((NX - 1,)),
+            dma((2, NY - 1)), dma((2, NY - 1)),
+            dma((2, NX - 1)), dma((2, NX - 1)),
             dma, dma,
         ],
         compiler_params=pltpu.CompilerParams(

time: 86.7 us -> 82.4 us (0.950)
  Pallas kernels: 82.9 us -> 78.3 us
    pallas_call x1, Pallas kernels: 82.9 us -> 78.3 us  [per_device(): pl.pallas_call(kernel, out_shape=jax.ShapeDtypeStruct((ROWS, VW), bf16),...]
where the time goes in v3:
time: 82.4 us; the launch traced here: 81.8 us
  Pallas kernels  78.3 us (95%)
  local copies, waits for them, and re-layouts  3.56 us (4%)
    pallas_call x1, Pallas kernels, per_device(): pl.pallas_call(kernel, out_shape=jax.ShapeDtypeStruct((ROWS, VW), bf16),...  78.3 us
    unnamed x7, local copies, waits for them, and re-layouts  3.56 us

profile of v3, /device:TPU:1, one launch (start us, length us, event | category | flops | bytes accessed | tf_op | source)
XLA Modules:
  0.0 81.8 jit_solution(8637285660117619826)
XLA Ops:
  0.0 0.0 copy-start
  0.0 1.1 %copy-done = bf16[2048,160]{0,1:T(8,128)(2,1)S(1)} copy-done((bf16[2048,160]{0,1:T(8,128)(2,1)S(1)}, bf16[2048,160]{0,1:T(8,128)(2,1)}, u32[]{:S(2)}) %copy-start) | copy-done | bytes 655384
  1.1 0.0 copy-start.1
  1.1 1.0 %copy-done.1 = bf16[128,2048]{1,0:T(8,128)(2,1)S(1)} copy-done((bf16[128,2048]{1,0:T(8,128)(2,1)S(1)}, bf16[128,2048]{1,0:T(8,128)(2,1)}, u32[]{:S(2)}) %copy-start.1) | copy-done | bytes 524312
  2.1 0.0 copy-start.2
  2.1 0.7 copy-done.2
  2.8 78.3 %fused.1 = bf16[1536,128]{1,0:T(8,128)(2,1)S(1)} custom-call(bf16[128,2048]{1,0:T(8,128)(2,1)S(1)} %copy-done.1, bf16[160,2048]{1,0:T(8,128)(2,1)S(1)} %bitcast.1, f32[4,160]{1,0:T(4,128)S(1)} %copy-done.2), custom_call_target="tpu_custom_call" | custom-call | tf_op jit(solution)/shard_map/fused/pallas_call | solution.py:430
  81.1 0.7 copy.5
Async XLA Ops:
  0.0 1.1 %copy-start = (bf16[2048,160]{0,1:T(8,128)(2,1)S(1)}, bf16[2048,160]{0,1:T(8,128)(2,1)}, u32[]{:S(2)}) copy-start(bf16[2048,160]{0,1:T(8,128)(2,1)} %param.4) | copy-start | bytes 1966084
  1.1 1.0 %copy-start.1 = (bf16[128,2048]{1,0:T(8,128)(2,1)S(1)}, bf16[128,2048]{1,0:T(8,128)(2,1)}, u32[]{:S(2)}) copy-start(bf16[128,2048]{1,0:T(8,128)(2,1)} %tok_ref.1) | copy-start | bytes 1572868
  2.1 0.7 copy-start.2

commit v4 on v3

--- a/solution.py
+++ b/solution.py
@@ -27,7 +27,7 @@
 
 
 def kernel(tok_ref, proj_ref, conv_ref, out_ref,
-           tokbuf, wr, wx, stage, xr, cw, vt, fq, fk, st, loc, px, ch, ybuf, tx, xbuf, pb, snd, fin, num, den,
+           own_w, taps, in_sem, tokbuf, wr, wx, stage, xr, cw, vt, fq, fk, st, loc, px, ch, ybuf, tx, xbuf, pb, snd, fin, num, den,
            tk_s, tk_r, zr_s, zr_r, zx_s, zx_r, xs_s, xs_r, ya_s, ya_r, yb_s, yb_r, xb_s, xb_r, at_s, at_r, h_s, h_r,
            d1_s, d1_r, sy_s, sy_r, sx_s, sx_r, d2_s, d2_r):
     c = lax.axis_index("ctx")
@@ -55,6 +55,13 @@
         return pltpu.make_async_remote_copy(
             src_ref=src, dst_ref=dst, send_sem=ss, recv_sem=rs, device_id=dev, device_id_type=MESH)
 
+    load_tok = pltpu.make_async_copy(tok_ref, tokbuf.at[zpar * 2 + r], in_sem.at[0])
+    load_w = pltpu.make_async_copy(proj_ref, own_w, in_sem.at[1])
+    load_taps = pltpu.make_async_copy(conv_ref, taps, in_sem.at[2])
+    load_tok.start()
+    load_w.start()
+    load_taps.start()
+
     barrier = pltpu.get_barrier_semaphore()
 
     def greet(dev):
@@ -73,8 +80,10 @@
     def _():
         greet((c - 1, z))
 
-    tokbuf[zpar * 2 + r] = tok_ref[...]
-    ca = conv_ref[...]
+    load_tok.wait()
+    load_w.wait()
+    load_taps.wait()
+    ca = taps[...]
     ca = jnp.concatenate([ca, ca], axis=0)
     taps_qk = ca[:, 0:128].T
     taps_v = ca[:, 32:WIDTH].T
@@ -100,14 +109,14 @@
     partner = at(x, y, 1 - r, z)
     own_tok = tokbuf.at[zpar * 2 + r]
     far_tok = tokbuf.at[(1 - zpar) * 2 + r]
-    tok_near = copy(tok_ref, own_tok, tk_s.at[0], tk_r.at[0], partner)
-    tok_pair = copy(tok_ref, own_tok, tk_s.at[1], tk_r.at[1], at(x, y, r, zpair))
+    tok_near = copy(own_tok, own_tok, tk_s.at[0], tk_r.at[0], partner)
+    tok_pair = copy(own_tok, own_tok, tk_s.at[1], tk_r.at[1], at(x, y, r, zpair))
     tok_relay = copy(far_tok, far_tok, tk_s.at[2], tk_r.at[2], partner)
 
     rhalf = pl.ds(pl.multiple_of(xpar * 80, 16), 80)
     xhalf = pl.ds(pl.multiple_of(ypar * 128, 128), 128)
-    rpiece = proj_ref.at[rhalf, pl.ds(pl.multiple_of(y * 128, 128), 128)]
-    xpiece = proj_ref.at[:, pl.ds(pl.multiple_of(1024 + x * 256 + ypar * 128, 128), 128)]
+    rpiece = own_w.at[rhalf, pl.ds(pl.multiple_of(y * 128, 128), 128)]
+    xpiece = own_w.at[:, pl.ds(pl.multiple_of(1024 + x * 256 + ypar * 128, 128), 128)]
     zr, zx, xs, yb, ring, xb = {}, {}, {}, {}, {}, {}
     for i in range(3):
         d = dist(i)
@@ -140,8 +149,8 @@
 
     def first(i):
         xs[i].wait_recv()
-        ring[i, 0, 1].start()
-        ring[i, 1, 1].start()
+        for way in range(2):
+            ring[i, way, 1].start()
         yb[i].wait_recv()
         for dx in range(1, NX):
             xb[i, dx].start()
@@ -173,7 +182,7 @@
         return block
 
     def from_own(j):
-        return proj_ref[:, j * 256:(j + 1) * 256]
+        return own_w[:, j * 256:(j + 1) * 256]
 
     tiles = {}
     for i in range(3):
@@ -192,49 +201,50 @@
         tiles[2, half, 0].start()
         xr[plane + 1] = stage[2, 2 * half + 1]
 
-    slots = range(3)
-    for i in slots:
-        guard(i, lambda i=i: z_start(i))
+    def third(body):
+        pl.when(r == 0)(body)
+
+    z_start(0)
+    tok_pair.start()
     tok_near.start()
+    z_start(1)
+    third(lambda: z_start(2))
     small(0)
-    tok_pair.start()
+    first(0)
     small(1)
-    guard(2, lambda: small(2))
-    for i in slots:
-        guard(i, lambda i=i: first(i))
-    for n in range(2, 5):
-        for i in slots:
-            guard(i, lambda i=i: step(i, n))
+    third(lambda: small(2))
+    step(0, 2)
+    first(1)
+    step(0, 3)
+    step(1, 2)
+    third(lambda: first(2))
+    step(0, 4)
+    step(1, 3)
+    third(lambda: step(2, 2))
     tok_near.wait_recv()
-    for i in range(2):
-        gathered(i)
-        work(i, 0)
+    gathered(0)
+    work(0, 0)
+    step(1, 4)
+    third(lambda: step(2, 3))
+    tok_pair.wait_recv()
+    tok_relay.start()
+    gathered(1)
+    work(1, 0)
+    third(lambda: step(2, 4))
+    tok_relay.wait_recv()
+    work(0, 1)
+    work(1, 1)
 
     @pl.when(r == 0)
     def _():
         gathered(2)
         work(2, 0)
-
-    tok_pair.wait_recv()
-    tok_relay.start()
+        work(2, 1)
 
     @pl.when(r == 1)
     def _():
         work_own(0, z)
-
-    tok_relay.wait_recv()
-    for i in range(2):
-        work(i, 1)
-
-    @pl.when(r == 0)
-    def _():
-        work(2, 1)
-
-    @pl.when(r == 1)
-    def _():
         work_own(1, zpair)
-
-    last = NZ - 1
 
     def tile_in(t):
         @pl.when(jnp.logical_or(r == 0, z // 2 != t // 2))
@@ -243,15 +253,6 @@
 
     def halo(dev):
         return copy(xr.at[NZ], xr.at[0], h_s, h_r, (dev, z))
-
-    tile_in(last)
-
-    @pl.when(c < 2 * NX * NY - 1)
-    def _():
-        halo(c + 1).start()
-
-    for t in range(last):
-        tile_in(t)
 
     lane = lax.broadcasted_iota(jnp.int32, (WIDTH, TILE), 1)
     quad = 1.0 / (2.0 ** 0.5 * FEAT ** 0.5)
@@ -277,9 +278,22 @@
         fq[rows, :] = features(acc[0:FEAT], 2.0).T.astype(bf16)
         fk[t] = features(acc[FEAT:2 * FEAT], 1.0).astype(bf16)
 
-    @pl.loop(1, NZ)
-    def _(t):
-        convolve(t)
+    a = 2 * (z // 2 + 2 + zpar)
+    for pairs, ready in (((0, 1), (1, 2, 3)), ((-1, 2), (-1, 0, 4, 5)), ((-2, 3), (-4, -3, -2, 6, 7))):
+        here = [lax.rem(a + 2 * p + q + NZ, NZ) for p in pairs for q in range(2)]
+        for t in here:
+            tile_in(t)
+
+        @pl.when(jnp.logical_and(c < 2 * NX * NY - 1, jnp.logical_or(here[1] == NZ - 1, here[3] == NZ - 1)))
+        def _():
+            halo(c + 1).start()
+
+        for n in ready:
+            t = lax.rem(a + n + NZ, NZ)
+
+            @pl.when(t != 0)
+            def _():
+                convolve(t)
 
     @pl.when(c == 0)
     def _():
@@ -430,9 +444,12 @@
     return pl.pallas_call(
         kernel,
         out_shape=jax.ShapeDtypeStruct((ROWS, VW), bf16),
-        in_specs=[pl.BlockSpec(memory_space=vmem)] * 3,
+        in_specs=[pl.BlockSpec(memory_space=pl.ANY)] * 3,
         out_specs=pl.BlockSpec(memory_space=vmem),
         scratch_shapes=[
+            vmem((WIDTH, D), bf16),
+            vmem((4, WIDTH), f32),
+            dma((3,)),
             vmem((4, TILE, D), bf16),
             vmem((3, NY, WIDTH, 128), bf16),
             vmem((3, NX, WIDTH, 256), bf16),
@@ -469,7 +486,7 @@
             dma, dma,
         ],
         compiler_params=pltpu.CompilerParams(
-            collective_id=0, has_side_effects=True, vmem_limit_bytes=48 * 2**20),
+            collective_id=0, has_side_effects=True, vmem_limit_bytes=60 * 2**20),
         name="fused",
     )(tokens, projection.T, conv_weight)
 

time: 82.4 us -> 84.7 us (1.028)
  Pallas kernels: 78.3 us -> 82.7 us
  local copies, waits for them, and re-layouts: 3.56 us -> 1.77 us
    pallas_call x1, Pallas kernels: 78.3 us -> 82.7 us  [per_device(): pl.pallas_call(kernel, out_shape=jax.ShapeDtypeStruct((ROWS, VW), bf16),...]
    unnamed x7 -> x1, local copies, waits for them, and re-layouts: 3.56 us -> 1.77 us
where the time goes in v4:
time: 84.7 us; the launch traced here: 84.5 us
  Pallas kernels  82.7 us (98%)
  local copies, waits for them, and re-layouts  1.77 us (2%)
    pallas_call x1, Pallas kernels, per_device(): pl.pallas_call(kernel, out_shape=jax.ShapeDtypeStruct((ROWS, VW), bf16),...  82.7 us
    unnamed x1, local copies, waits for them, and re-layouts  1.77 us

profile of v4, /device:TPU:1, one launch (start us, length us, event | category | flops | bytes accessed | tf_op | source)
XLA Modules:
  0.0 84.5 jit_solution(13596235675485426683)
XLA Ops:
  0.0 82.7 %fused.1 = bf16[1536,128]{1,0:T(8,128)(2,1)} custom-call(bf16[128,2048]{1,0:T(8,128)(2,1)} %tok_ref.1, bf16[160,2048]{1,0:T(8,128)(2,1)} %bitcast.1, f32[4,160]{1,0:T(4,128)} %conv_ref.1), custom_call_target="tpu_custom_call" | custom-call | tf_op jit(solution)/shard_map/fused/pallas_call | solution.py:444
  82.8 1.8 %copy.5 = bf16[1536,128]{1,0:T(8,128)(2,1)} copy(bf16[1536,128]{1,0:T(8,128)(2,1)} %fused.1) | data formatting | bytes 786432

commit v5 on v4

--- a/solution.py
+++ b/solution.py
@@ -8,6 +8,8 @@
 NX, NY, NZ = 4, 8, 12
 D = 2048
 FEAT = 16
+KY = D // 4
+KX = (D - KY) // NX
 VW = 128
 WIDTH = 2 * FEAT + VW
 TILE = 128
@@ -28,14 +30,13 @@
 
 def kernel(tok_ref, proj_ref, conv_ref, out_ref,
            own_w, taps, in_sem, tokbuf, wr, wx, stage, xr, cw, vt, fq, fk, st, loc, px, ch, ybuf, tx, xbuf, pb, snd, fin, num, den,
-           tk_s, tk_r, zr_s, zr_r, zx_s, zx_r, xs_s, xs_r, ya_s, ya_r, yb_s, yb_r, xb_s, xb_r, at_s, at_r, h_s, h_r,
+           tk_s, tk_r, zr_s, zr_r, zx_s, zx_r, ya_s, ya_r, yb_s, yb_r, xb_s, xb_r, at_s, at_r, h_s, h_r,
            d1_s, d1_r, sy_s, sy_r, sx_s, sx_r, d2_s, d2_r):
     c = lax.axis_index("ctx")
     z = lax.axis_index("tp")
     r = lax.rem(c, 2)
     y = lax.rem(c // 2, NY)
     x = c // (2 * NY)
-    xpar = lax.rem(x, 2)
     ypar = lax.rem(y, 2)
     zpar = lax.rem(z, 2)
 
@@ -113,76 +114,63 @@
     tok_pair = copy(own_tok, own_tok, tk_s.at[1], tk_r.at[1], at(x, y, r, zpair))
     tok_relay = copy(far_tok, far_tok, tk_s.at[2], tk_r.at[2], partner)
 
-    rhalf = pl.ds(pl.multiple_of(xpar * 80, 16), 80)
-    xhalf = pl.ds(pl.multiple_of(ypar * 128, 128), 128)
-    rpiece = own_w.at[rhalf, pl.ds(pl.multiple_of(y * 128, 128), 128)]
-    xpiece = own_w.at[:, pl.ds(pl.multiple_of(1024 + x * 256 + ypar * 128, 128), 128)]
-    zr, zx, xs, yb, ring, xb = {}, {}, {}, {}, {}, {}
+    rows = pl.ds(pl.multiple_of(ypar * 80, 16), 80)
+    xlanes = pl.ds(pl.multiple_of(KY + x * KX, 128), KX)
+    zr, zx, yb, ya, xb = {}, {}, {}, {}, {}
     for i in range(3):
         d = dist(i)
         to = at(x, y, r, zo(d * (1 - 2 * lax.rem(z + d, 2))))
-        zr[i] = copy(rpiece, wr.at[i, y, rhalf, :], zr_s.at[i], zr_r.at[i], to)
-        zx[i] = copy(xpiece, wx.at[i, x, :, xhalf], zx_s.at[i], zx_r.at[i], to)
-        ref = wr.at[i, y, rhalf, :]
-        xs[i] = copy(ref, ref, xs_s.at[i], xs_r.at[i], at(x + 1 - 2 * xpar, y, r, z))
-        ref = wx.at[i, x, :, xhalf]
-        yb[i] = copy(ref, ref, yb_s.at[i], yb_r.at[i], at(x, y + 1 - 2 * ypar, r, z))
+        block = wr.at[i, y // 2, rows, :]
+        zr[i] = copy(own_w.at[rows, pl.ds(pl.multiple_of(y // 2 * 128, 128), 128)], block, zr_s.at[i], zr_r.at[i], to)
+        for dy in range(1, NY):
+            ya[i, dy] = copy(block, block, ya_s.at[i, dy - 1], ya_r.at[i, dy - 1], at(x, yo(dy), r, z))
+        block = wx.at[i, x, rows, :]
+        zx[i] = copy(own_w.at[rows, xlanes], block, zx_s.at[i], zx_r.at[i], to)
+        yb[i] = copy(block, block, yb_s.at[i], yb_r.at[i], at(x, y + 1 - 2 * ypar, r, z))
+        block = wx.at[i, x]
         for dx in range(1, NX):
-            ref = wx.at[i, x]
-            xb[i, dx] = copy(ref, ref, xb_s.at[i, dx - 1], xb_r.at[i, dx - 1], at(xo(dx), y, r, z))
-        for s in range(1, 5):
-            for way, sign in ((0, 1), (1, -1)):
-                ref = wr.at[i, yo(-sign * (s - 1))]
-                if s == 4:
-                    ref = wr.at[i, yo(-sign * 3), pl.ds(80 * way, 80), :]
-                ring[i, way, s] = copy(ref, ref, ya_s.at[i, way, s - 1], ya_r.at[i, way, s - 1], at(x, yo(sign), r, z))
+            xb[i, dx] = copy(block, block, xb_s.at[i, dx - 1], xb_r.at[i, dx - 1], at(xo(dx), y, r, z))
 
     def z_start(i):
         zr[i].start()
         zx[i].start()
 
     def small(i):
-        zr[i].wait_recv()
-        xs[i].start()
         zx[i].wait_recv()
         yb[i].start()
-
-    def first(i):
-        xs[i].wait_recv()
-        for way in range(2):
-            ring[i, way, 1].start()
+        zr[i].wait_recv()
+        for dy in (4, 3, 5, 2, 6, 1, 7):
+            ya[i, dy].start()
+
+    def large(i):
         yb[i].wait_recv()
-        for dx in range(1, NX):
+        for dx in (2, 1, 3):
             xb[i, dx].start()
-
-    def step(i, s):
-        for way in range(2):
-            ring[i, way, s - 1].wait_recv()
-            ring[i, way, s].start()
 
     def gathered(i):
         for dx in range(1, NX):
             xb[i, dx].wait_recv()
-        for way in range(2):
-            ring[i, way, 4].wait_recv()
+        for dy in range(1, NY):
+            ya[i, dy].wait_recv()
 
     def project(i, half, block):
         first_set = 2 * (zpar if half == 0 else 1 - zpar)
         acc = jnp.zeros((WIDTH, 2 * TILE), f32)
-        for j in range(8):
-            acc = acc + dot_nt(block(j), tokbuf[pl.ds(first_set, 2), :, j * 256:(j + 1) * 256].reshape(2 * TILE, 256))
+        for j in range(6):
+            k = slice(j * 256, (j + 1) * 256) if j < 2 else slice(KY + (j - 2) * KX, KY + (j - 1) * KX)
+            acc = acc + dot_nt(block(j, k), tokbuf[pl.ds(first_set, 2), :, k].reshape(2 * TILE, k.stop - k.start))
         for q in range(2):
             stage[i, 2 * half + q] = acc[:, q * TILE:(q + 1) * TILE].astype(bf16)
 
     def from_gather(i):
-        def block(j):
-            if j < 4:
+        def block(j, k):
+            if j < 2:
                 return jnp.concatenate([wr[i, 2 * j], wr[i, 2 * j + 1]], axis=1)
-            return wx[i, j - 4]
+            return wx[i, j - 2]
         return block
 
-    def from_own(j):
-        return own_w[:, j * 256:(j + 1) * 256]
+    def from_own(j, k):
+        return own_w[:, k]
 
     tiles = {}
     for i in range(3):
@@ -205,34 +193,25 @@
         pl.when(r == 0)(body)
 
     z_start(0)
-    tok_pair.start()
-    tok_near.start()
     z_start(1)
     third(lambda: z_start(2))
+    tok_near.start()
     small(0)
-    first(0)
+    tok_pair.start()
+    large(0)
     small(1)
     third(lambda: small(2))
-    step(0, 2)
-    first(1)
-    step(0, 3)
-    step(1, 2)
-    third(lambda: first(2))
-    step(0, 4)
-    step(1, 3)
-    third(lambda: step(2, 2))
+    large(1)
+    third(lambda: large(2))
     tok_near.wait_recv()
     gathered(0)
     work(0, 0)
-    step(1, 4)
-    third(lambda: step(2, 3))
     tok_pair.wait_recv()
     tok_relay.start()
+    tok_relay.wait_recv()
+    work(0, 1)
     gathered(1)
     work(1, 0)
-    third(lambda: step(2, 4))
-    tok_relay.wait_recv()
-    work(0, 1)
     work(1, 1)
 
     @pl.when(r == 0)
@@ -414,13 +393,11 @@
     def left(i):
         zr[i].wait_send()
         zx[i].wait_send()
-        xs[i].wait_send()
         yb[i].wait_send()
         for dx in range(1, NX):
             xb[i, dx].wait_send()
-        for way in range(2):
-            for s in range(1, 5):
-                ring[i, way, s].wait_send()
+        for dy in range(1, NY):
+            ya[i, dy].wait_send()
         for half in range(2):
             tiles[i, half, 1].wait_send()
 
@@ -451,8 +428,8 @@
             vmem((4, WIDTH), f32),
             dma((3,)),
             vmem((4, TILE, D), bf16),
-            vmem((3, NY, WIDTH, 128), bf16),
-            vmem((3, NX, WIDTH, 256), bf16),
+            vmem((3, KY // 128, WIDTH, 128), bf16),
+            vmem((3, NX, WIDTH, KX), bf16),
             vmem((3, 4, WIDTH, TILE), bf16),
             vmem((NZ + 1, WIDTH, TILE), bf16),
             vmem((4, WIDTH, TILE), f32),
@@ -474,8 +451,7 @@
             dma((3,)), dma((3,)),
             dma((3,)), dma((3,)),
             dma((3,)), dma((3,)),
-            dma((3,)), dma((3,)),
-            dma((3, 2, 4)), dma((3, 2, 4)),
+            dma((3, NY - 1)), dma((3, NY - 1)),
             dma((3,)), dma((3,)),
             dma((3, NX - 1)), dma((3, NX - 1)),
             dma((3, 4)), dma((NZ,)),
@@ -486,7 +462,7 @@
             dma, dma,
         ],
         compiler_params=pltpu.CompilerParams(
-            collective_id=0, has_side_effects=True, vmem_limit_bytes=60 * 2**20),
+            collective_id=0, has_side_effects=True, vmem_limit_bytes=107 * 2**19),
         name="fused",
     )(tokens, projection.T, conv_weight)
 

time: 84.7 us -> 76.6 us (0.904)
  Pallas kernels: 82.7 us -> 75 us
    pallas_call x1, Pallas kernels: 82.7 us -> 75 us  [per_device(): pl.pallas_call(kernel, out_shape=jax.ShapeDtypeStruct((ROWS, VW), bf16),...]
    unnamed x1 -> x3, local copies, waits for them, and re-layouts: 1.77 us -> 1.43 us
where the time goes in v5:
time: 76.6 us; the launch traced here: 76.5 us
  Pallas kernels  75 us (98%)
  local copies, waits for them, and re-layouts  1.43 us (2%)
    pallas_call x1, Pallas kernels, per_device(): pl.pallas_call(kernel, out_shape=jax.ShapeDtypeStruct((ROWS, VW), bf16),...  75 us

profile of v5, /device:TPU:1, one launch (start us, length us, event | category | flops | bytes accessed | tf_op | source)
XLA Modules:
  0.0 76.5 jit_solution(1945995528957543080)
XLA Ops:
  0.0 0.0 copy-start
  0.0 0.7 copy-done
  0.7 75.0 %fused.1 = bf16[1536,128]{1,0:T(8,128)(2,1)S(1)} custom-call(bf16[128,2048]{1,0:T(8,128)(2,1)} %tok_ref.1, bf16[160,2048]{1,0:T(8,128)(2,1)} %bitcast.1, f32[4,160]{1,0:T(4,128)S(1)} %copy-done), custom_call_target="tpu_custom_call" | custom-call | tf_op jit(solution)/shard_map/fused/pallas_call | solution.py:421
  75.7 0.7 copy.5
Async XLA Ops:
  0.0 0.7 copy-start

commit v6 on v5

--- a/solution.py
+++ b/solution.py
@@ -81,17 +81,6 @@
     def _():
         greet((c - 1, z))
 
-    load_tok.wait()
-    load_w.wait()
-    load_taps.wait()
-    ca = taps[...]
-    ca = jnp.concatenate([ca, ca], axis=0)
-    taps_qk = ca[:, 0:128].T
-    taps_v = ca[:, 32:WIDTH].T
-    for o in range(4):
-        cw[o, 0:32] = jnp.broadcast_to(taps_qk[0:32, o:o + 1], (32, 128))
-        cw[o, 32:] = jnp.broadcast_to(taps_v[:, o:o + 1], (VW, 128))
-
     pl.semaphore_wait(barrier, NX + NY - 1 + 2 * (NZ - 1) + r * (1 - c // (2 * NX * NY - 1)))
 
     way_z = 2 * zpar - 1
@@ -132,8 +121,8 @@
             xb[i, dx] = copy(block, block, xb_s.at[i, dx - 1], xb_r.at[i, dx - 1], at(xo(dx), y, r, z))
 
     def z_start(i):
+        zx[i].start()
         zr[i].start()
-        zx[i].start()
 
     def small(i):
         zx[i].wait_recv()
@@ -192,10 +181,20 @@
     def third(body):
         pl.when(r == 0)(body)
 
+    load_w.wait()
     z_start(0)
     z_start(1)
     third(lambda: z_start(2))
+    load_tok.wait()
     tok_near.start()
+    load_taps.wait()
+    ca = taps[...]
+    ca = jnp.concatenate([ca, ca], axis=0)
+    taps_qk = ca[:, 0:128].T
+    taps_v = ca[:, 32:WIDTH].T
+    for o in range(4):
+        cw[o, 0:32] = jnp.broadcast_to(taps_qk[0:32, o:o + 1], (32, 128))
+        cw[o, 32:] = jnp.broadcast_to(taps_v[:, o:o + 1], (VW, 128))
     small(0)
     tok_pair.start()
     large(0)
@@ -324,9 +323,9 @@
     def to_y(src, dst, ss, rs):
         out = []
         for d in range(1, NY):
-            cp = copy(src(d), dst.at[d - 1], ss.at[d - 1], rs.at[d - 1], at(x, yo(d), r, z))
-            cp.start()
-            out.append(cp)
+            out.append(copy(src(d), dst.at[d - 1], ss.at[d - 1], rs.at[d - 1], at(x, yo(d), r, z)))
+        for d in (4, 3, 5, 2, 6, 1, 7):
+            out[d - 1].start()
         sends.extend(out)
         return out
 

time: 76.6 us -> 76.4 us (level)
  no operation moved by 1% of the time
where the time goes in v6:
time: 76.4 us; the launch traced here: 76.2 us
  Pallas kernels  74.8 us (98%)
  local copies, waits for them, and re-layouts  1.43 us (2%)
    pallas_call x1, Pallas kernels, per_device(): pl.pallas_call(kernel, out_shape=jax.ShapeDtypeStruct((ROWS, VW), bf16),...  74.8 us

profile of v6, /device:TPU:1, one launch (start us, length us, event | category | flops | bytes accessed | tf_op | source)
XLA Modules:
  0.0 76.2 jit_solution(10385324220812766896)
XLA Ops:
  0.0 0.0 copy-start
  0.0 0.7 copy-done
  0.7 74.8 %fused.1 = bf16[1536,128]{1,0:T(8,128)(2,1)S(1)} custom-call(bf16[128,2048]{1,0:T(8,128)(2,1)} %tok_ref.1, bf16[160,2048]{1,0:T(8,128)(2,1)} %bitcast.1, f32[4,160]{1,0:T(4,128)S(1)} %copy-done), custom_call_target="tpu_custom_call" | custom-call | tf_op jit(solution)/shard_map/fused/pallas_call | solution.py:420
  75.5 0.7 copy.5
Async XLA Ops:
  0.0 0.7 copy-start

commit v7 on v5

--- a/solution.py
+++ b/solution.py
@@ -330,13 +330,15 @@
         sends.extend(out)
         return out
 
+    x_sends = []
+
     def to_x(src, dst, ss, rs):
         out = []
         for d in range(1, NX):
             cp = copy(src, dst.at[d - 1], ss.at[d - 1], rs.at[d - 1], at(xo(d), y, r, z))
-            cp.start()
+            pl.when(x + d < NX)(cp.start)
             out.append(cp)
-        sends.extend(out)
+            x_sends.append((d, cp))
         return out
 
     x_second = to_x(ch.at[1], xbuf.at[1], sx_s.at[1], sx_r.at[1])
@@ -344,7 +346,7 @@
     within(0)
     second = jnp.zeros((PART, 128), f32)
     for d in range(1, NX):
-        x_second[d - 1].wait_recv()
+        pl.when(x >= d)(x_second[d - 1].wait_recv)
         second = second + jnp.where(x >= d, xbuf[1, d - 1], 0.0)
     pb[0] = second
     pb[1] = second + ch[1]
@@ -363,7 +365,7 @@
         y_second[d - 1].wait_recv()
         second = second + ybuf[1, d - 1]
     for d in range(1, NX):
-        x_first[d - 1].wait_recv()
+        pl.when(x >= d)(x_first[d - 1].wait_recv)
         first_rows = first_rows + jnp.where(x >= d, xbuf[0, d - 1], 0.0)
     before = jnp.concatenate([first_rows, second], axis=0)
     snd[...] = before + jnp.where(r == 0, loc[mine, :], 0.0)
@@ -409,6 +411,8 @@
         cp.wait_send()
     for cp in sends:
         cp.wait_send()
+    for d, cp in x_sends:
+        pl.when(x + d < NX)(cp.wait_send)
 
     @pl.when(c < 2 * NX * NY - 1)
     def _():

time: 76.6 us -> 75.5 us (0.986)
  Pallas kernels: 75 us -> 73.3 us
    pallas_call x1, Pallas kernels: 75 us -> 73.3 us  [per_device(): pl.pallas_call(kernel, out_shape=jax.ShapeDtypeStruct((ROWS, VW), bf16),...]
where the time goes in v7:
time: 75.5 us; the launch traced here: 74.8 us
  Pallas kernels  73.3 us (97%)
  local copies, waits for them, and re-layouts  1.43 us (2%)
    pallas_call x1, Pallas kernels, per_device(): pl.pallas_call(kernel, out_shape=jax.ShapeDtypeStruct((ROWS, VW), bf16),...  73.3 us

profile of v7, /device:TPU:1, one launch (start us, length us, event | category | flops | bytes accessed | tf_op | source)
XLA Modules:
  0.0 74.8 jit_solution(12093935676835969438)
XLA Ops:
  0.0 0.0 copy-start
  0.0 0.7 copy-done
  0.7 73.3 %fused.1 = bf16[1536,128]{1,0:T(8,128)(2,1)S(1)} custom-call(bf16[128,2048]{1,0:T(8,128)(2,1)} %tok_ref.1, bf16[160,2048]{1,0:T(8,128)(2,1)} %bitcast.1, f32[4,160]{1,0:T(4,128)S(1)} %copy-done), custom_call_target="tpu_custom_call" | custom-call | tf_op jit(solution)/shard_map/fused/pallas_call | solution.py:425
  74.0 0.7 %copy.5 = bf16[1536,128]{1,0:T(8,128)(2,1)} copy(bf16[1536,128]{1,0:T(8,128)(2,1)S(1)} %fused.1) | data formatting | bytes 786432
Async XLA Ops:
  0.0 0.7 copy-start

commit v8 on v7

--- a/solution.py
+++ b/solution.py
@@ -324,9 +324,9 @@
     def to_y(src, dst, ss, rs):
         out = []
         for d in range(1, NY):
-            cp = copy(src(d), dst.at[d - 1], ss.at[d - 1], rs.at[d - 1], at(x, yo(d), r, z))
-            cp.start()
-            out.append(cp)
+            out.append(copy(src(d), dst.at[d - 1], ss.at[d - 1], rs.at[d - 1], at(x, yo(d), r, z)))
+        for d in (4, 3, 5, 2, 6, 1, 7):
+            out[d - 1].start()
         sends.extend(out)
         return out
 
@@ -341,8 +341,8 @@
             x_sends.append((d, cp))
         return out
 
+    y_first = to_y(lambda d: ch.at[0], ybuf.at[0], sy_s.at[0], sy_r.at[0])
     x_second = to_x(ch.at[1], xbuf.at[1], sx_s.at[1], sx_r.at[1])
-    y_first = to_y(lambda d: ch.at[0], ybuf.at[0], sy_s.at[0], sy_r.at[0])
     within(0)
     second = jnp.zeros((PART, 128), f32)
     for d in range(1, NX):

time: 75.5 us -> 74.9 us (level)
  no operation moved by 1% of the time
where the time goes in v8:
time: 74.9 us; the launch traced here: 74.7 us
  Pallas kernels  73.2 us (98%)
  local copies, waits for them, and re-layouts  1.43 us (2%)
    pallas_call x1, Pallas kernels, per_device(): pl.pallas_call(kernel, out_shape=jax.ShapeDtypeStruct((ROWS, VW), bf16),...  73.2 us

profile of v8, /device:TPU:1, one launch (start us, length us, event | category | flops | bytes accessed | tf_op | source)
XLA Modules:
  0.0 74.7 jit_solution(17488391271102782705)
XLA Ops:
  0.0 0.0 copy-start
  0.0 0.7 copy-done
  0.7 73.2 %fused.1 = bf16[1536,128]{1,0:T(8,128)(2,1)S(1)} custom-call(bf16[128,2048]{1,0:T(8,128)(2,1)} %tok_ref.1, bf16[160,2048]{1,0:T(8,128)(2,1)} %bitcast.1, f32[4,160]{1,0:T(4,128)S(1)} %copy-done), custom_call_target="tpu_custom_call" | custom-call | tf_op jit(solution)/shard_map/fused/pallas_call | solution.py:425
  73.9 0.7 %copy.5 = bf16[1536,128]{1,0:T(8,128)(2,1)} copy(bf16[1536,128]{1,0:T(8,128)(2,1)S(1)} %fused.1) | data formatting | bytes 786432
Async XLA Ops:
  0.0 0.7 copy-start
